TPU v7x, 256 devices: a whole 4x4x8 slice. The times are simulated.
256 devices in a mesh: ctx: 16 (over y, x_lo, core), tp: 16 (over x_hi, z).
Axes of the slice: x: 4 (x_hi: 2, x_lo: 2; x = x_hi * 2 + x_lo), y: 4, z: 8, core: 2. Of those that a mesh axis runs over, the one named last changes fastest.
Arguments:
- inputs: bfloat16 [2048, 4096], P('ctx', 'tp'), may hold values from -6 to 6
- w_in: bfloat16 [4096, 3, 4096], P(None, None, 'tp'), may hold values from -0.125 to 0.125
- conv_taps: float32 [3, 3, 4096], P(None, None, 'tp'), may hold values from -3 to 3
- pole_rates: float32 [4096, 16], P('tp'), may hold values from 4.8828125e-05 to 0.0333333333
- residues: float32 [4096, 16], P('tp'), may hold values from -2.5 to 2.5
- cotangent: bfloat16 [2048, 4096], P('ctx', 'tp'), may hold values from -6 to 6
Outputs:
- grad_inputs: bfloat16 [2048, 4096], P('ctx', 'tp')
All inputs are finite; a program needn't handle non-finite values.
Results may differ from a plain program's by a relative error of at most 0.024.
Values may be sent and summed in bfloat16 or wider, within the bound.
A program may use at most 128 MiB of HBM per device.

v0:
```python
import jax
import jax.numpy as jnp
from jax import lax
from jax.sharding import PartitionSpec as P

HIGH = lax.Precision.HIGHEST


def shifted(block, axis, distance):
    devices = range(lax.axis_size(axis))
    route = [(i - distance, i) for i in devices if i - distance in devices]
    return lax.ppermute(block, axis, route)


def powers(rate_t, offsets):
    return jnp.exp(-rate_t[:, None, :] * offsets[None, :, None])


def body(inputs, w_in, conv_taps, pole_rates, residues, cotangent):
    tok_rows = inputs.shape[0]
    width = w_in.shape[0]
    channels = w_in.shape[2]
    w_flat = w_in.reshape(width, 3 * channels)
    proj_sum = jnp.dot(
        lax.all_gather(inputs, "tp", axis=1, tiled=True), w_flat, preferred_element_type=jnp.float32
    )
    projected = proj_sum.astype(jnp.bfloat16).reshape(tok_rows, 3, channels)
    earlier_rim = shifted(projected[tok_rows - 2 :], "ctx", 1)
    padded = jnp.concatenate([earlier_rim, projected], axis=0).astype(jnp.float32)
    filtered = (
        conv_taps[0] * padded[2:]
        + conv_taps[1] * padded[1 : tok_rows + 1]
        + conv_taps[2] * padded[0:tok_rows]
    )
    gate = filtered[:, 0]
    key_part = filtered[:, 1]
    value_part = filtered[:, 2]
    mixing = key_part * value_part
    rate_t = pole_rates.T
    res_t = residues.T
    in_gain = jnp.sqrt(-jnp.expm1(-2.0 * rate_t))
    out_gain = res_t * in_gain
    blk_rows = min(128, tok_rows)
    blk_count = tok_rows // blk_rows
    offsets = jnp.arange(blk_rows, dtype=jnp.float32)
    decays = powers(rate_t, offsets)
    kern_vals = jnp.einsum("nc,nkc->kc", out_gain, decays, precision=HIGH)
    distance = jnp.arange(blk_rows)[:, None] - jnp.arange(blk_rows)[None, :]
    toeplitz = jnp.where(
        (distance >= 0)[:, :, None], kern_vals[jnp.clip(distance, 0, blk_rows - 1)], 0.0
    )
    lam_blk = jnp.exp(-rate_t * blk_rows)
    carry_fwd = res_t[:, None, :] * powers(rate_t, offsets + 1.0)
    end_fwd = in_gain[:, None, :] * powers(rate_t, blk_rows - 1.0 - offsets)
    carry_bwd = out_gain[:, None, :] * powers(rate_t, blk_rows - offsets)

    def forward_block(carried, block_in):
        local = jnp.einsum("tsc,sc->tc", toeplitz, block_in, precision=HIGH)
        local = local + jnp.einsum("ntc,nc->tc", carry_fwd, carried, precision=HIGH)
        carried = lam_blk * carried + jnp.einsum("nsc,sc->nc", end_fwd, block_in, precision=HIGH)
        return (carried, local)

    def backward_block(carried, block_in):
        local = jnp.einsum("tsc,tc->sc", toeplitz, block_in, precision=HIGH)
        local = local + jnp.einsum("nsc,nc->sc", carry_bwd, carried, precision=HIGH)
        carried = lam_blk * carried + jnp.einsum("ntc,tc->nc", decays, block_in, precision=HIGH)
        return (carried, local)

    zero_state = jnp.zeros(rate_t.shape, jnp.float32)
    grads_out = cotangent.astype(jnp.float32)
    grad_long = grads_out * gate
    start_adj, adj_local = lax.scan(
        backward_block, zero_state, grad_long.reshape(blk_count, blk_rows, channels), reverse=True
    )
    end_state, long_local = lax.scan(
        forward_block, zero_state, mixing.reshape(blk_count, blk_rows, channels)
    )
    lam_shard = jnp.exp(-rate_t * tok_rows)

    def relay_forward(turn, carried):
        incoming = shifted(carried[0], "ctx", 1)
        return (lam_shard * incoming + end_state, incoming)

    def relay_backward(turn, carried):
        incoming = shifted(carried[0], "ctx", -1)
        return (lam_shard * incoming + start_adj, incoming)

    entry_fwd = lax.fori_loop(0, lax.axis_size("ctx"), relay_forward, (end_state, zero_state))[1]
    entry_bwd = lax.fori_loop(0, lax.axis_size("ctx"), relay_backward, (start_adj, zero_state))[1]
    row_offsets = jnp.arange(tok_rows, dtype=jnp.float32)
    long_out = long_local.reshape(tok_rows, channels) + jnp.einsum(
        "ntc,nc->tc",
        res_t[:, None, :] * powers(rate_t, row_offsets + 1.0),
        entry_fwd,
        precision=HIGH,
    )
    grad_mixing = adj_local.reshape(tok_rows, channels) + jnp.einsum(
        "nsc,nc->sc",
        out_gain[:, None, :] * powers(rate_t, tok_rows - row_offsets),
        entry_bwd,
        precision=HIGH,
    )
    grad_gate = grads_out * long_out
    grad_filtered = jnp.stack([grad_gate, grad_mixing * value_part, grad_mixing * key_part], axis=1)
    later_rim = shifted(grad_filtered[:2], "ctx", -1)
    padded_grad = jnp.concatenate([grad_filtered, later_rim], axis=0)
    grad_projected = (
        (
            conv_taps[0] * padded_grad[0:tok_rows]
            + conv_taps[1] * padded_grad[1 : tok_rows + 1]
            + conv_taps[2] * padded_grad[2 : tok_rows + 2]
        )
        .astype(jnp.bfloat16)
        .reshape(tok_rows, 3 * channels)
    )
    partial_terms = lax.dot_general(
        grad_projected, w_flat, (((1,), (1,)), ((), ())), preferred_element_type=jnp.float32
    )
    summed = lax.psum(partial_terms.astype(jnp.bfloat16), "tp").astype(jnp.float32)
    owned = lax.dynamic_slice_in_dim(summed, lax.axis_index("tp") * channels, channels, 1)
    return owned.astype(jnp.bfloat16)


def solution(mesh):
    in_specs = (
        P("ctx", "tp"),
        P(None, None, "tp"),
        P(None, None, "tp"),
        P("tp", None),
        P("tp", None),
        P("ctx", "tp"),
    )
    out_specs = P("ctx", "tp")
    return jax.shard_map(body, mesh=mesh, in_specs=in_specs, out_specs=out_specs, check_vma=False)
```

profile of v0, /device:TPU:8, one launch (start us, length us, event | category | flops | bytes accessed | tf_op | source)
XLA Modules:
  0.0 627.5 jit_solution(131137259146892803)
XLA Ops:
  7.3 8.8 %copy.10 = bf16[4096,3,256]{0,2,1:T(8,128)(2,1)} copy(bf16[4096,3,256]{2,0,1:T(8,128)(2,1)} %param.11) | data formatting | bytes 12582912 | tf_op args[1]
  16.2 72.0 %all-gather.2.cloned.1.call-done = bf16[128,4096]{1,0:T(8,128)(2,1)} async-done(((bf16[128,256]{1,0:T(8,128)(2,1)}), bf16[128,4096]{1,0:T(8,128)(2,1)}) %all-gather.2.cloned.1.call-update) | async-done | bytes 1048592 | tf_op jit(solution)/shard_map/all_gather | solution.py:25
  88.2 5.4 convolution_convert_fusion
  102.2 102.1 %while.5 = (s32[]{:T(128)}, f32[16,256]{1,0:T(8,128)S(1)}, f32[16,256]{1,0:T(8,128)}, f32[16,256]{1,0:T(8,128)S(1)}, f32[16,256]{1,0:T(8,128)S(1)}, /*index=5*/s32[]{:T(128)}) while((s32[]{:T(128)}, f32[16,256]{1,0:T(8,128)S(1)}, f32[16,256]{1,0:T(8,128)}, f32[16,256]{1,0:T(8,128)S(1)}, f32[16,256]{1,0:T(8,128)S(1)}, ...), condition=%wide.region_3.4_spmd, body=%wide.region_2.3_spmd.sunk | while | flops 8194 | bytes 196745 | solution.py:89
  106.1 4.5 collective-permute-start.1
  112.7 4.5 collective-permute-start.1
  119.2 4.5 collective-permute-start.1
  125.8 4.5 collective-permute-start.1
  132.3 4.5 collective-permute-start.1
  138.8 4.5 collective-permute-start.1
  145.4 4.5 collective-permute-start.1
  158.5 4.5 collective-permute-start.1
  171.6 4.5 collective-permute-start.1
  184.7 4.5 collective-permute-start.1
  197.7 4.5 collective-permute-start.1
  204.9 104.8 %while.4 = (s32[]{:T(128)}, f32[16,256]{1,0:T(8,128)S(1)}, f32[16,256]{1,0:T(8,128)}, f32[16,256]{1,0:T(8,128)S(1)}, f32[16,256]{1,0:T(8,128)S(1)}, /*index=5*/s32[]{:T(128)}) while((s32[]{:T(128)}, f32[16,256]{1,0:T(8,128)S(1)}, f32[16,256]{1,0:T(8,128)}, f32[16,256]{1,0:T(8,128)S(1)}, f32[16,256]{1,0:T(8,128)S(1)}, ...), condition=%wide.region_1.2_spmd, body=%wide.region_0.1_spmd.sunk | while | flops 8194 | bytes 196745 | solution.py:88
  312.1 61.8 %gather_fusion = f32[16384,256]{1,0:T(8,128)} fusion(f32[128,256]{1,0:T(8,128)S(1)} %bitcast.106, s32[16384]{0:T(1024)S(1)} %fusion.15), kind=kCustom, calls=%fused_computation | custom fusion | bytes 33619968 | tf_op jit(solution)/shard_map/gather | solution.py:50
  373.9 12.2 %broadcast_select_fusion = f32[128,128,256]{2,1,0:T(8,128)} fusion(f32[128,128,256]{2,1,0:T(8,128)} %bitcast.107, pred[128,128]{1,0:T(8,128)(4,1)S(1)} %subtract_compare_fusion), kind=kLoop, calls=%fused_computation.3 | loop fusion | flops 4194304 | bytes 33570816 | tf_op jit(solution)/shard_map/jit(_where)/select_n | solution.py:49
  386.1 18.0 %copy.44 = f32[128,128,256]{1,0,2:T(8,128)} copy(f32[128,128,256]{2,1,0:T(8,128)} %broadcast_select_fusion) | data formatting | bytes 33554432 | tf_op jit(solution)/shard_map/jit(_where)/select_n | solution.py:49
  404.3 29.4 %fusion.16 = f32[256,1,128]{2,1,0:T(1,128)S(1)} fusion(f32[128,256,1]{0,2,1:T(1,128)S(1)} %bitcast.112, f32[128,128,256]{1,0,2:T(8,128)} %copy.44), kind=kOutput, calls=%fused_computation.62 | convolution fusion | flops 50331648 | bytes 17039360 | tf_op jit(solution)/shard_map/while/body/eval_jaxpr/tsc,sc->tc/dot_general | solution.py:58
  433.8 14.7 %fusion.17 = f32[256,1,128]{2,1,0:T(1,128)S(1)} fusion(f32[128,256,1]{0,2,1:T(1,128)S(1)} %bitcast.110, f32[128,128,256]{1,0,2:T(8,128)S(1)} %copy-done), kind=kOutput, calls=%fused_computation.63 | convolution fusion | flops 50331648 | bytes 17039360 | tf_op jit(solution)/shard_map/while/body/eval_jaxpr/tsc,tc->sc/dot_general | solution.py:64
  450.7 5.3 collective-permute-done.3
  456.0 6.6 %fusion = bf16[128,4096]{1,0:T(8,128)(2,1)} fusion(bf16[4096,3,256]{2,0,1:T(8,128)(2,1)} %param.11, f32[130,3,256]{0,2,1:T(8,128)S(1)} %pad_maximum_fusion, f32[3,256]{1,0:T(4,128)S(1)} %get-tuple-element.147, f32[3,256]{1,0:T(4,128)S(1)} %get-tuple-element.148, f32[3,256]{1,0:T(4,128)S(1)} %get-tuple-element.146, ...), kind=kOutput, calls=%fused_computation.5 | convolution fusion | flops 806617088 | bytes 8141824 | tf_op jit(solution)/shard_map/dot_general | solution.py:116
  462.6 156.6 %all-reduce.2.cloned.1.call-done = bf16[128,4096]{1,0:T(8,128)(2,1)} async-done(((bf16[128,4096]{1,0:T(8,128)(2,1)}), bf16[128,4096]{1,0:T(8,128)(2,1)}) %all-reduce.2.cloned.1.call-update) | async-done | bytes 1048592 | tf_op jit(solution)/shard_map/psum | solution.py:119
  (198 shorter events, 173.1 us)
Async XLA Ops:
  6.5 81.7 %all-gather.2.cloned.1.call-start = ((), (), s32[]{:S(2)}) async-start(), calls=%async_computation | async-start | bytes 1114112 | tf_op jit(solution)/shard_map/all_gather | solution.py:25
  7.3 611.9 %all-reduce.2.cloned.1.call-start = ((), (), s32[]{:S(2)}) async-start(), calls=%async_computation.1 | async-start | bytes 2097152 | tf_op jit(solution)/shard_map/psum | solution.py:119
  106.1 5.9 collective-permute-start.1
  112.7 5.9 collective-permute-start.1
  119.2 5.9 collective-permute-start.1
  125.8 5.9 collective-permute-start.1
  132.3 5.9 collective-permute-start.1
  138.8 5.9 collective-permute-start.1
  145.4 5.9 collective-permute-start.1
  151.9 5.9 collective-permute-start.1
  158.5 5.9 collective-permute-start.1
  165.0 5.9 collective-permute-start.1
  171.6 5.9 collective-permute-start.1
  178.1 5.9 collective-permute-start.1
  184.7 5.9 collective-permute-start.1
  191.2 5.9 collective-permute-start.1
  197.7 5.9 collective-permute-start.1
  211.4 5.9 collective-permute-start
  218.0 5.9 collective-permute-start
  224.6 5.9 collective-permute-start
  231.1 5.9 collective-permute-start
  237.7 5.9 collective-permute-start
  244.2 5.9 collective-permute-start
  448.8 7.2 %collective-permute-start.3 = (f32[2,3,256]{0,2,1:T(8,128)S(1)}, f32[2,3,256]{0,2,1:T(8,128)S(1)}, u32[]{:S(2)}, u32[]{:S(2)}) collective-permute-start(f32[2,3,256]{0,2,1:T(8,128)S(1)} %bitcast.118), channel_id=1, source_target_pairs={{16,0},{32,16},{48,32},{64,48},{80,64},{96,80},{112,96},{128,112},... | collective-permute-start | bytes 18440 | tf_op jit(solution)/shard_map/ppermute | solution.py:12
  (49 other events, 144.1 us)
Sparse Core Ops, SparseCore 0:
  9.8 78.3 all-gather.1
  462.8 156.3 all-reduce.1
where the time goes:
time: 629 us; the launch traced here: 628 us
  waiting for transfers between devices  325 us (52%)
  local copies, waits for them, and re-layouts  110 us (17%)
  starting transfers between devices  104 us (17%)
  matrix products  56.1 us (9%)
  other arithmetic  18.1 us (3%)
  between operations  13.7 us (2%)
    psum x1, waiting for transfers between devices, body(): lax.psum(partial_terms.astype(jnp.bfloat16), 'tp').astype(jnp.float32)  157 us
    ppermute x34, starting transfers between devices, shifted(): return lax.ppermute(block, axis, route)  104 us
    ppermute x34, waiting for transfers between devices, shifted(): return lax.ppermute(block, axis, route)  96.1 us
    all_gather x1, waiting for transfers between devices, body(): lax.all_gather(inputs, 'tp', axis=1, tiled=True)  72 us
    gather x1, local copies, waits for them, and re-layouts, body(): kern_vals[jnp.clip(distance, 0, blk_rows - 1)]  61.8 us
    dot_general x1, matrix products, forward_block(): local = jnp.einsum('tsc,sc->tc', toeplitz, block_in, precision=HIGH)  29.4 us
    while x64, local copies, waits for them, and re-layouts  19 us
    select_n x1, local copies, waits for them, and re-layouts, body(): jnp.where((distance >= 0)[:, :, None], kern_vals[jnp.clip(distance, 0, bl...  18 us
  transfers between devices with their start and end apart: 36, of which 36 were waited for; matrix products, arithmetic and copies ran while one was open for 1% of the time, Pallas kernels for 0%

commit v1 on v0

v1 whole, which is shorter than its diff:
```python
import functools

import jax
import jax.numpy as jnp
from jax import lax
from jax.experimental import pallas as pl
from jax.experimental.pallas import tpu as pltpu
from jax.sharding import PartitionSpec as P

MESH = pl.DeviceIdType.MESH
F32 = jnp.float32
BF16 = jnp.bfloat16
SUB = 8
LANES = 128
COLUMNS = 2


def one_minus_exp(x):
    series = jnp.ones_like(x)
    for k in range(9, 1, -1):
        series = 1.0 - x * series * (1.0 / k)
    return jnp.where(x < 0.25, x * series, 1.0 - jnp.exp(-x))


def kernel(
    n_ctx,
    n_tp,
    x_hbm,
    w_hbm,
    taps_hbm,
    rate_hbm,
    res_hbm,
    cot_hbm,
    out_hbm,
    w,
    xg,
    taps,
    rate,
    res,
    cot,
    proj,
    gate,
    keyp,
    valp,
    mixp,
    glp,
    fwd_pow,
    rev_pow,
    kern,
    spread,
    gain,
    w_fwd,
    w_bwd,
    part,
    state,
    state_in,
    rim,
    gfp,
    sliding,
    long_out,
    grad_mix,
    gp,
    rs_out,
    rs_in,
    x_out,
    x_in,
    result,
    local_sem,
    w_sem,
    g_send,
    g_recv,
    s_send,
    s_recv,
    rim_send,
    rim_recv,
    r_send,
    r_recv,
):
    rows, chans = x_hbm.shape
    poles = rate_hbm.shape[0]
    ring = n_tp // COLUMNS
    far, near = (ring - 1 + 1) // 2, (ring - 1) // 2
    streams = ((0, 1, far), (0, -1, near), (1, 1, near), (1, -1, far))
    ctx = lax.axis_index("ctx")
    tp = lax.axis_index("tp")
    col, z = tp // ring, tp % ring

    def at_z(column, zz):
        return column * ring + (zz + 2 * ring) % ring

    partner = at_z(1 - col, z)
    neighbour = {1: at_z(col, z + 1), -1: at_z(col, z - 1)}
    next_ctx = lax.rem(ctx + 1, n_ctx)
    prev_ctx = lax.rem(ctx + n_ctx - 1, n_ctx)

    barrier = pltpu.get_barrier_semaphore()
    for other in (neighbour[1], neighbour[-1], partner):
        pl.semaphore_signal(barrier, inc=1, device_id=(ctx, other), device_id_type=MESH)

    def greet(o, _):
        pl.semaphore_signal(barrier, inc=1, device_id=(lax.rem(ctx + o, n_ctx), tp), device_id_type=MESH)
        return 0

    lax.fori_loop(1, n_ctx, greet, 0)

    w_copies = [pltpu.make_async_copy(w_hbm.at[j], w.at[j], w_sem.at[j]) for j in range(3)]
    small = [
        pltpu.make_async_copy(src, dst, local_sem.at[i])
        for i, (src, dst) in enumerate(
            ((x_hbm, xg.at[tp]), (taps_hbm, taps), (rate_hbm, rate), (res_hbm, res), (cot_hbm, cot))
        )
    ]
    for c in small + w_copies:
        c.start()
    pl.semaphore_wait(barrier, 3 + n_ctx - 1)

    def remote(src, dst, send, recv, device):
        return pltpu.make_async_remote_copy(
            src_ref=src, dst_ref=dst, send_sem=send, recv_sem=recv, device_id=device, device_id_type=MESH
        )

    def g_copy(k, s, slot, src=None):
        here = xg.at[slot]
        return remote(here if src is None else src, here, g_send.at[k, s], g_recv.at[k, s], (ctx, neighbour[streams[k][1]]))

    def x_pair(slot, src):
        return remote(src, xg.at[slot], g_send.at[4, 0], g_recv.at[4, 0], (ctx, partner))

    x_pair(tp, x_hbm).start()
    g_copy(0, 1, tp, x_hbm).start()
    g_copy(1, 1, tp, x_hbm).start()

    for c in small[1:]:
        c.wait()

    rates = rate[...]
    gain[...] = jnp.sqrt(one_minus_exp(2.0 * rates))
    kern[...] = jnp.zeros_like(kern)
    steps = lax.broadcasted_iota(jnp.int32, (rows, chans), 0).astype(F32)
    state_in[ctx] = jnp.zeros(state_in.shape[1:], BF16)

    def tables(n, _):
        r = rate[pl.ds(n, 1), :]
        up = jnp.exp(-r * steps)
        fwd_pow[n] = up
        rev_pow[n] = jnp.exp(-r * (rows - 1.0 - steps))
        kern[...] += up * (res[pl.ds(n, 1), :] * gain[pl.ds(n, 1), :])
        return 0

    def state_weights(i, _):
        gap = (jnp.abs(ctx - i) - 1) * rows
        weight = jnp.exp(-rate[...] * gap.astype(F32))
        w_fwd[i] = jnp.where(i < ctx, weight, 0.0)
        w_bwd[i] = jnp.where(i > ctx, weight, 0.0)
        return 0

    def project(slot):
        block = xg[slot]
        start = pl.multiple_of(slot * chans, chans)

        def branch(j, _):
            proj[j, SUB:, :] += jnp.dot(block, w[j, pl.ds(start, chans), :], preferred_element_type=F32)
            return 0

        lax.fori_loop(0, 3, branch, 0)

    proj[...] = jnp.zeros_like(proj)
    small[0].wait()
    for c in w_copies:
        c.wait()
    project(tp)
    x_pair(partner, xg.at[partner]).wait_recv()
    g_copy(2, 1, partner).start()
    g_copy(3, 1, partner).start()
    project(partner)
    per_step = -(-poles // far)
    ctx_per_step = -(-n_ctx // far)

    def gather_step(s, _):
        for k, (c, d, hops) in enumerate(streams):
            slot = at_z(col if c == 0 else 1 - col, z - s * d)

            @pl.when(s <= hops)
            def _(k=k, slot=slot, hops=hops):
                g_copy(k, s, slot).wait_recv()

                @pl.when(s < hops)
                def _():
                    g_copy(k, s + 1, slot).start()

                project(slot)

        lax.fori_loop((s - 1) * per_step, jnp.minimum(s * per_step, poles), tables, 0)
        lax.fori_loop((s - 1) * ctx_per_step, jnp.minimum(s * ctx_per_step, n_ctx), state_weights, 0)
        return 0

    lax.fori_loop(1, far + 1, gather_step, 0)

    def spread_rows(i, _):
        block = kern[pl.ds(pl.multiple_of(SUB * i, SUB), SUB), :]
        for r in range(SUB):
            spread[SUB * i + r] = jnp.broadcast_to(block[r : r + 1, :], (SUB, chans))
        return 0

    lax.fori_loop(0, rows // SUB, spread_rows, 0)

    for j in range(3):
        proj[j, SUB:, :] = proj[j, SUB:, :].astype(BF16).astype(F32)
    rim1 = remote(proj.at[:, pl.ds(rows, SUB), :], rim.at[0], rim_send.at[0], rim_recv.at[0], (next_ctx, tp))
    rim1.start()

    def filter_rows(lo, n):
        out = []
        for j in range(3):
            acc = taps[0, j : j + 1, :] * proj[j, SUB + lo : SUB + lo + n, :]
            acc += taps[1, j : j + 1, :] * proj[j, SUB + lo - 1 : SUB + lo + n - 1, :]
            acc += taps[2, j : j + 1, :] * proj[j, SUB + lo - 2 : SUB + lo + n - 2, :]
            out.append(acc)
        gate[lo : lo + n, :] = out[0]
        keyp[lo : lo + n, :] = out[1]
        valp[lo : lo + n, :] = out[2]
        mixp[SUB + lo : SUB + lo + n, :] = out[1] * out[2]
        glp[lo : lo + n, :] = cot[...].astype(F32)[lo : lo + n] * out[0]

    mixp[0:SUB, :] = jnp.zeros((SUB, chans), F32)
    glp[rows : rows + SUB, :] = jnp.zeros((SUB, chans), F32)
    filter_rows(SUB, rows - SUB)

    def partial_states(n, _):
        fwd = rev_pow[n, SUB:, :] * mixp[2 * SUB :, :]
        bwd = fwd_pow[n, SUB:, :] * glp[SUB:rows, :]
        part[0, n] = jnp.sum(fwd.reshape(rows // SUB - 1, SUB, chans), axis=0)
        part[1, n] = jnp.sum(bwd.reshape(rows // SUB - 1, SUB, chans), axis=0)
        return 0

    lax.fori_loop(0, poles, partial_states, 0)
    rim1.wait()
    proj[:, 0:SUB, :] = jnp.where(ctx > 0, rim[0], 0.0)
    filter_rows(0, SUB)

    def last_states(n, _):
        part[0, n] += rev_pow[n, 0:SUB, :] * mixp[SUB : 2 * SUB, :]
        part[1, n] += fwd_pow[n, 0:SUB, :] * glp[0:SUB, :]
        return 0

    lax.fori_loop(0, poles, last_states, 0)
    state[0] = (gain[...] * jnp.sum(part[0], axis=1)).astype(BF16)
    state[1] = jnp.sum(part[1], axis=1).astype(BF16)

    def s_copy(o):
        other = lax.rem(ctx + o, n_ctx)
        which = (other < ctx).astype(jnp.int32)
        return remote(state.at[which], state_in.at[ctx], s_send.at[o], s_recv.at[o], (other, tp))

    def send_state(o, _):
        s_copy(o).start()
        return 0

    lax.fori_loop(1, n_ctx, send_state, 0)

    tiles = rows // SUB

    def local_conv(which, flip, store):
        for lane in range(0, chans, LANES):
            cols = slice(lane, lane + LANES)

            def tap(r, acc, cols=cols):
                acc = list(acc)
                block = [sliding[which, r, SUB * i : SUB * i + SUB, cols] for i in range(tiles)]
                for m in range(tiles):
                    k = spread[SUB * m + r, :, cols]
                    for i in range(tiles - m):
                        if flip:
                            acc[i + m] = acc[i + m] + k * block[i]
                        else:
                            acc[i] = acc[i] + k * block[i + m]
                return tuple(acc)

            acc = lax.fori_loop(0, SUB, tap, (jnp.zeros((SUB, LANES), F32),) * tiles)
            for i in range(tiles):
                store[SUB * i : SUB * i + SUB, cols] = acc[i]

    for r in range(SUB):
        sliding[0, r] = mixp[SUB - r : SUB - r + rows, :]
        sliding[1, r] = glp[r : r + rows, :]
    local_conv(0, True, long_out)
    local_conv(1, False, grad_mix)

    def wait_state(o, _):
        s_copy(o).wait()
        return 0

    lax.fori_loop(1, n_ctx, wait_state, 0)

    def add_state(i, carried):
        got = state_in[i].astype(F32)
        return carried[0] + w_fwd[i] * got, carried[1] + w_bwd[i] * got

    none = jnp.zeros((poles, chans), F32)
    before, after = lax.fori_loop(0, n_ctx, add_state, (none, none))
    decayed = res[...] * jnp.exp(-rates)
    part[0, :, 0, :] = decayed * before
    part[1, :, 0, :] = decayed * gain[...] * after

    def finish_rows(lo, n):
        def add_fwd(p, acc):
            return acc + fwd_pow[p, lo : lo + n, :] * part[0, p, 0:1, :]

        def add_bwd(p, acc):
            return acc + rev_pow[p, lo : lo + n, :] * part[1, p, 0:1, :]

        whole = lax.fori_loop(0, poles, add_fwd, long_out[lo : lo + n, :])
        gfp[0, lo : lo + n, :] = cot[...].astype(F32)[lo : lo + n] * whole
        whole = lax.fori_loop(0, poles, add_bwd, grad_mix[lo : lo + n, :])
        gfp[1, lo : lo + n, :] = whole * valp[lo : lo + n, :]
        gfp[2, lo : lo + n, :] = whole * keyp[lo : lo + n, :]

    finish_rows(0, SUB)
    rim2 = remote(gfp.at[:, pl.ds(0, SUB), :], rim.at[1], rim_send.at[1], rim_recv.at[1], (prev_ctx, tp))
    rim2.start()
    finish_rows(SUB, rows - SUB)
    rim2.wait()
    gfp[:, rows : rows + SUB, :] = jnp.where(ctx < n_ctx - 1, rim[1], 0.0)
    for j in range(3):
        acc = taps[0, j : j + 1, :] * gfp[j, 0:rows, :]
        acc += taps[1, j : j + 1, :] * gfp[j, 1 : rows + 1, :]
        acc += taps[2, j : j + 1, :] * gfp[j, 2 : rows + 2, :]
        gp[j] = acc.astype(BF16)

    def partial_of(slot):
        start = pl.multiple_of(slot * chans, chans)

        def branch(j, acc):
            return acc + lax.dot_general(
                gp[j], w[j, pl.ds(start, chans), :], (((1,), (1,)), ((), ())), preferred_element_type=F32
            )

        return lax.fori_loop(0, 3, branch, jnp.zeros((rows, chans), F32))

    def r_copy(k, s):
        return remote(rs_out.at[k, s], rs_in.at[k, s], r_send.at[k, s], r_recv.at[k, s], (ctx, neighbour[streams[k][1]]))

    order = (3, 2, 0, 1)

    def reduce_step(s, _):
        for k in order:
            c, d, hops = streams[k]
            slot = at_z(col if c == 0 else 1 - col, z + (hops - s) * d)

            @pl.when(s < hops)
            def _(k=k, slot=slot):
                rs_out[k, s] = partial_of(slot).astype(BF16)

                @pl.when(s > 0)
                def _():
                    r_copy(k, s - 1).wait_recv()
                    rs_out[k, s] = (rs_out[k, s].astype(F32) + rs_in[k, s - 1].astype(F32)).astype(BF16)

                r_copy(k, s).start()

        return 0

    lax.fori_loop(0, far, reduce_step, 0)
    long_out[...] = partial_of(partner)
    for k in (2, 3):
        r_copy(k, streams[k][2] - 1).wait_recv()
        long_out[...] += rs_in[k, streams[k][2] - 1].astype(F32)
    x_out[...] = long_out[...].astype(BF16)
    swap = remote(x_out, x_in, r_send.at[4, 0], r_recv.at[4, 0], (ctx, partner))
    swap.start()
    long_out[...] = partial_of(tp)
    for k in (0, 1):
        r_copy(k, streams[k][2] - 1).wait_recv()
        long_out[...] += rs_in[k, streams[k][2] - 1].astype(F32)
    swap.wait_recv()
    result[...] = (long_out[...] + x_in[...].astype(F32)).astype(BF16)
    done = pltpu.make_async_copy(result, out_hbm, local_sem.at[0])
    done.start()

    swap.wait_send()
    x_pair(tp, x_hbm).wait_send()
    for k, (c, d, hops) in enumerate(streams):

        def left(s, _, k=k):
            g_copy(k, s, tp).wait_send()
            r_copy(k, s - 1).wait_send()
            return 0

        lax.fori_loop(1, hops + 1, left, 0)
    done.wait()


def body(n_ctx, n_tp, inputs, w_in, conv_taps, pole_rates, residues, cotangent):
    rows, chans = inputs.shape
    width = w_in.shape[0]
    poles = pole_rates.shape[1]
    far = n_tp // COLUMNS // 2
    vmem = pltpu.VMEM
    dma = pltpu.SemaphoreType.DMA
    scratch = [
        vmem((3, width, chans), BF16),
        vmem((n_tp, rows, chans), BF16),
        vmem((3, 3, chans), F32),
        vmem((poles, chans), F32),
        vmem((poles, chans), F32),
        vmem((rows, chans), BF16),
        vmem((3, rows + SUB, chans), F32),
        vmem((rows, chans), F32),
        vmem((rows, chans), F32),
        vmem((rows, chans), F32),
        vmem((rows + SUB, chans), F32),
        vmem((rows + SUB, chans), F32),
        vmem((poles, rows, chans), F32),
        vmem((poles, rows, chans), F32),
        vmem((rows, chans), F32),
        vmem((rows, SUB, chans), F32),
        vmem((poles, chans), F32),
        vmem((n_ctx, poles, chans), F32),
        vmem((n_ctx, poles, chans), F32),
        vmem((2, poles, SUB, chans), F32),
        vmem((2, poles, chans), BF16),
        vmem((n_ctx, poles, chans), BF16),
        vmem((2, 3, SUB, chans), F32),
        vmem((3, rows + SUB, chans), F32),
        vmem((2, SUB, rows, chans), F32),
        vmem((rows, chans), F32),
        vmem((rows, chans), F32),
        vmem((3, rows, chans), BF16),
        vmem((4, far, rows, chans), BF16),
        vmem((4, far, rows, chans), BF16),
        vmem((rows, chans), BF16),
        vmem((rows, chans), BF16),
        vmem((rows, chans), BF16),
        dma((5,)),
        dma((3,)),
        dma((5, far + 1)),
        dma((5, far + 1)),
        dma((n_ctx,)),
        dma((n_ctx,)),
        dma((2,)),
        dma((2,)),
        dma((5, far)),
        dma((5, far)),
    ]
    return pl.pallas_call(
        functools.partial(kernel, n_ctx, n_tp),
        out_shape=jax.ShapeDtypeStruct((rows, chans), BF16),
        in_specs=[pl.BlockSpec(memory_space=pl.ANY)] * 6,
        out_specs=pl.BlockSpec(memory_space=pl.ANY),
        scratch_shapes=scratch,
        compiler_params=pltpu.CompilerParams(
            collective_id=0, has_side_effects=True, vmem_limit_bytes=60 * 1024 * 1024
        ),
        cost_estimate=pl.CostEstimate(
            flops=4 * rows * width * 3 * chans, bytes_accessed=2 * 3 * width * chans, transcendentals=0
        ),
        name="hyena_input_grad",
    )(inputs, w_in.transpose(1, 0, 2), conv_taps, pole_rates.T, residues.T, cotangent)


def solution(mesh):
    in_specs = (
        P("ctx", "tp"),
        P(None, None, "tp"),
        P(None, None, "tp"),
        P("tp", None),
        P("tp", None),
        P("ctx", "tp"),
    )
    out_specs = P("ctx", "tp")
    step = functools.partial(body, mesh.shape["ctx"], mesh.shape["tp"])
    return jax.shard_map(step, mesh=mesh, in_specs=in_specs, out_specs=out_specs, check_vma=False)
```

time: 629 us -> 60.6 us (0.10)
  waiting for transfers between devices: 325 us -> 0 us
  local copies, waits for them, and re-layouts: 110 us -> 1.47 us
  starting transfers between devices: 104 us -> 0 us
  Pallas kernels: 0 us -> 58.4 us
  matrix products: 56.1 us -> 0 us
  other arithmetic: 18.1 us -> 0 us
  between operations: 13.7 us -> 0.01 us
    psum x1 -> x0, waiting for transfers between devices: 157 us -> none  [body(): lax.psum(partial_terms.astype(jnp.bfloat16), 'tp').astype(jnp.float32)]
    ppermute x34 -> x0, starting transfers between devices: 104 us -> none  [shifted(): return lax.ppermute(block, axis, route)]
    ppermute x34 -> x0, waiting for transfers between devices: 96.1 us -> none  [shifted(): return lax.ppermute(block, axis, route)]
    all_gather x1 -> x0, waiting for transfers between devices: 72 us -> none  [body(): lax.all_gather(inputs, 'tp', axis=1, tiled=True)]
    gather x1 -> x0, local copies, waits for them, and re-layouts: 61.8 us -> none  [body(): kern_vals[jnp.clip(distance, 0, blk_rows - 1)]]
    pallas_call x0 -> x1, Pallas kernels: none -> 58.4 us  [body(): pl.pallas_call(functools.partial(kernel, n_ctx, n_tp), out_shape=jax.Shap...]
    dot_general x4 -> x0, matrix products: 56.1 us -> none  [the longest x1 29.4 us: forward_block(): local = jnp.einsum('tsc,sc->tc', toeplitz, block_in, precision=HIGH)]
    while x64 -> x0, local copies, waits for them, and re-layouts: 19 us -> none
  transfers between devices with their start and end apart: 36 -> 0, of which waited for: 36 -> 0; matrix products, arithmetic and copies ran while one was open for 1% -> 0% of each run, Pallas kernels for 0% -> 0%
where the time goes in v1:
time: 60.6 us; the launch traced here: 59.9 us
  Pallas kernels  58.4 us (96%)
  local copies, waits for them, and re-layouts  1.47 us (2%)
    pallas_call x1, Pallas kernels, body(): pl.pallas_call(functools.partial(kernel, n_ctx, n_tp), out_shape=jax.Shap...  58.4 us
    unnamed x1, local copies, waits for them, and re-layouts  1.47 us

profile of v1, /device:TPU:8, one launch (start us, length us, event | category | flops | bytes accessed | tf_op | source)
XLA Modules:
  0.0 59.9 jit_solution(13859941392457077552)
XLA Ops:
  0.0 58.4 %hyena_input_grad.1 = bf16[128,256]{1,0:T(8,128)(2,1)} custom-call(bf16[128,256]{1,0:T(8,128)(2,1)} %x_hbm.1, bf16[3,4096,256]{2,1,0:T(8,128)(2,1)} %bitcast.3, f32[3,3,256]{2,1,0:T(4,128)} %taps_hbm.1, f32[16,256]{1,0:T(8,128)} %bitcast.4, f32[16,256]{1,0:T(8,128)} %bitcast.5, bf16[128,256]{1,0:T(8,128)(2,1)} %cot_hbm.1), custom_call_target="tpu_custom_call" | custom-call | flops 1610612736 | bytes 6291456 | tf_op jit(solution)/shard_map/hyena_input_grad/pallas_call | solution.py:445
  58.4 1.5 %copy.8 = bf16[128,256]{1,0:T(8,128)(2,1)} copy(bf16[128,256]{1,0:T(8,128)(2,1)} %hyena_input_grad.1) | data formatting | bytes 131072

commit v2 on v1

--- a/solution.py
+++ b/solution.py
@@ -12,6 +12,7 @@
 BF16 = jnp.bfloat16
 SUB = 8
 LANES = 128
+PIECES = 2
 COLUMNS = 2
 
 
@@ -47,19 +48,21 @@
     fwd_pow,
     rev_pow,
     kern,
+    kern_late,
     spread,
     gain,
     w_fwd,
     w_bwd,
     part,
+    ends,
     state,
     state_in,
-    rim,
     gfp,
     sliding,
     long_out,
     grad_mix,
     gp,
+    ready,
     rs_out,
     rs_in,
     x_out,
@@ -71,8 +74,6 @@
     g_recv,
     s_send,
     s_recv,
-    rim_send,
-    rim_recv,
     r_send,
     r_recv,
 ):
@@ -90,11 +91,10 @@
 
     partner = at_z(1 - col, z)
     neighbour = {1: at_z(col, z + 1), -1: at_z(col, z - 1)}
-    next_ctx = lax.rem(ctx + 1, n_ctx)
-    prev_ctx = lax.rem(ctx + n_ctx - 1, n_ctx)
+    diagonal = {1: at_z(1 - col, z + 1), -1: at_z(1 - col, z - 1)}
 
     barrier = pltpu.get_barrier_semaphore()
-    for other in (neighbour[1], neighbour[-1], partner):
+    for other in (neighbour[1], neighbour[-1], diagonal[1], diagonal[-1], partner):
         pl.semaphore_signal(barrier, inc=1, device_id=(ctx, other), device_id_type=MESH)
 
     def greet(o, _):
@@ -112,23 +112,32 @@
     ]
     for c in small + w_copies:
         c.start()
-    pl.semaphore_wait(barrier, 3 + n_ctx - 1)
+    pl.semaphore_wait(barrier, 5 + n_ctx - 1)
 
     def remote(src, dst, send, recv, device):
         return pltpu.make_async_remote_copy(
             src_ref=src, dst_ref=dst, send_sem=send, recv_sem=recv, device_id=device, device_id_type=MESH
         )
 
-    def g_copy(k, s, slot, src=None):
-        here = xg.at[slot]
-        return remote(here if src is None else src, here, g_send.at[k, s], g_recv.at[k, s], (ctx, neighbour[streams[k][1]]))
-
-    def x_pair(slot, src):
-        return remote(src, xg.at[slot], g_send.at[4, 0], g_recv.at[4, 0], (ctx, partner))
-
-    x_pair(tp, x_hbm).start()
-    g_copy(0, 1, tp, x_hbm).start()
-    g_copy(1, 1, tp, x_hbm).start()
+    size = rows // PIECES
+
+    def piece(p):
+        return pl.ds(p * size, size)
+
+    def g_copy(k, s, p, slot, src=None):
+        c, d, _ = streams[k]
+        here = xg.at[slot, piece(p)]
+        there = neighbour[d] if src is None or c == 0 else diagonal[d]
+        src = here if src is None else src.at[piece(p)]
+        return remote(src, here, g_send.at[k, s, p], g_recv.at[k, s, p], (ctx, there))
+
+    def x_pair(slot):
+        return remote(x_hbm, xg.at[slot], g_send.at[4, 0, 0], g_recv.at[4, 0, 0], (ctx, partner))
+
+    for p in range(PIECES):
+        for k in range(4):
+            g_copy(k, 1, p, tp, x_hbm).start()
+    x_pair(tp).start()
 
     for c in small[1:]:
         c.wait()
@@ -137,7 +146,7 @@
     gain[...] = jnp.sqrt(one_minus_exp(2.0 * rates))
     kern[...] = jnp.zeros_like(kern)
     steps = lax.broadcasted_iota(jnp.int32, (rows, chans), 0).astype(F32)
-    state_in[ctx] = jnp.zeros(state_in.shape[1:], BF16)
+    state_in[ctx, 0:poles] = jnp.zeros((poles, chans), BF16)
 
     def tables(n, _):
         r = rate[pl.ds(n, 1), :]
@@ -169,26 +178,32 @@
     for c in w_copies:
         c.wait()
     project(tp)
-    x_pair(partner, xg.at[partner]).wait_recv()
-    g_copy(2, 1, partner).start()
-    g_copy(3, 1, partner).start()
-    project(partner)
     per_step = -(-poles // far)
     ctx_per_step = -(-n_ctx // far)
 
     def gather_step(s, _):
-        for k, (c, d, hops) in enumerate(streams):
-            slot = at_z(col if c == 0 else 1 - col, z - s * d)
+        slots = [at_z(col if c == 0 else 1 - col, z - s * d) for c, d, _ in streams]
+        for p in range(PIECES):
+            for k, (_, _, hops) in enumerate(streams):
+
+                @pl.when(s <= hops)
+                def _(k=k, p=p, hops=hops):
+                    g_copy(k, s, p, slots[k]).wait_recv()
+
+                    @pl.when(s < hops)
+                    def _():
+                        g_copy(k, s + 1, p, slots[k]).start()
+
+        for k, (_, _, hops) in enumerate(streams):
 
             @pl.when(s <= hops)
-            def _(k=k, slot=slot, hops=hops):
-                g_copy(k, s, slot).wait_recv()
-
-                @pl.when(s < hops)
-                def _():
-                    g_copy(k, s + 1, slot).start()
-
-                project(slot)
+            def _(k=k):
+                project(slots[k])
+
+        @pl.when(s == min(2, far))
+        def _():
+            x_pair(partner).wait_recv()
+            project(partner)
 
         lax.fori_loop((s - 1) * per_step, jnp.minimum(s * per_step, poles), tables, 0)
         lax.fori_loop((s - 1) * ctx_per_step, jnp.minimum(s * ctx_per_step, n_ctx), state_weights, 0)
@@ -203,49 +218,45 @@
         return 0
 
     lax.fori_loop(0, rows // SUB, spread_rows, 0)
+    kern_late[0:1, :] = jnp.zeros((1, chans), F32)
+    kern_late[1:rows, :] = kern[0 : rows - 1, :]
 
     for j in range(3):
         proj[j, SUB:, :] = proj[j, SUB:, :].astype(BF16).astype(F32)
-    rim1 = remote(proj.at[:, pl.ds(rows, SUB), :], rim.at[0], rim_send.at[0], rim_recv.at[0], (next_ctx, tp))
-    rim1.start()
-
-    def filter_rows(lo, n):
-        out = []
-        for j in range(3):
-            acc = taps[0, j : j + 1, :] * proj[j, SUB + lo : SUB + lo + n, :]
-            acc += taps[1, j : j + 1, :] * proj[j, SUB + lo - 1 : SUB + lo + n - 1, :]
-            acc += taps[2, j : j + 1, :] * proj[j, SUB + lo - 2 : SUB + lo + n - 2, :]
-            out.append(acc)
-        gate[lo : lo + n, :] = out[0]
-        keyp[lo : lo + n, :] = out[1]
-        valp[lo : lo + n, :] = out[2]
-        mixp[SUB + lo : SUB + lo + n, :] = out[1] * out[2]
-        glp[lo : lo + n, :] = cot[...].astype(F32)[lo : lo + n] * out[0]
-
+    edge = [proj[j, SUB : SUB + 1, :] for j in range(3)] + [cot[0:16, :].astype(F32)[0:1]]
+    edge += [proj[j, SUB + 1 : SUB + 2, :] for j in range(3)] + [cot[0:16, :].astype(F32)[1:2]]
+    blank = jnp.zeros((1, chans), F32)
+    edge += [proj[j, SUB + rows - 2 : SUB + rows - 1, :] for j in range(3)] + [blank]
+    edge += [proj[j, SUB + rows - 1 : SUB + rows, :] for j in range(3)] + [blank]
+    edge = jnp.concatenate(edge, axis=0).astype(BF16)
+    for target in (state.at[0], state.at[1], state_in.at[ctx]):
+        target[poles:, :] = edge
+
+    filtered = []
+    for j in range(3):
+        acc = taps[0, j : j + 1, :] * proj[j, SUB : SUB + rows, :]
+        acc += taps[1, j : j + 1, :] * proj[j, SUB - 1 : SUB + rows - 1, :]
+        acc += taps[2, j : j + 1, :] * proj[j, SUB - 2 : SUB + rows - 2, :]
+        filtered.append(acc)
+    keyp[...] = filtered[1]
+    valp[...] = filtered[2]
     mixp[0:SUB, :] = jnp.zeros((SUB, chans), F32)
+    mixp[SUB:, :] = jnp.where(steps >= 2.0, filtered[1] * filtered[2], 0.0)
+    glp[0:rows, :] = jnp.where(steps >= 2.0, cot[...].astype(F32) * filtered[0], 0.0)
     glp[rows : rows + SUB, :] = jnp.zeros((SUB, chans), F32)
-    filter_rows(SUB, rows - SUB)
 
     def partial_states(n, _):
-        fwd = rev_pow[n, SUB:, :] * mixp[2 * SUB :, :]
-        bwd = fwd_pow[n, SUB:, :] * glp[SUB:rows, :]
-        part[0, n] = jnp.sum(fwd.reshape(rows // SUB - 1, SUB, chans), axis=0)
-        part[1, n] = jnp.sum(bwd.reshape(rows // SUB - 1, SUB, chans), axis=0)
+        fwd = rev_pow[n] * mixp[SUB:, :]
+        bwd = fwd_pow[n] * glp[0:rows, :]
+        part[0, n] = jnp.sum(fwd.reshape(rows // SUB, SUB, chans), axis=0)
+        part[1, n] = jnp.sum(bwd.reshape(rows // SUB, SUB, chans), axis=0)
         return 0
 
     lax.fori_loop(0, poles, partial_states, 0)
-    rim1.wait()
-    proj[:, 0:SUB, :] = jnp.where(ctx > 0, rim[0], 0.0)
-    filter_rows(0, SUB)
-
-    def last_states(n, _):
-        part[0, n] += rev_pow[n, 0:SUB, :] * mixp[SUB : 2 * SUB, :]
-        part[1, n] += fwd_pow[n, 0:SUB, :] * glp[0:SUB, :]
-        return 0
-
-    lax.fori_loop(0, poles, last_states, 0)
-    state[0] = (gain[...] * jnp.sum(part[0], axis=1)).astype(BF16)
-    state[1] = jnp.sum(part[1], axis=1).astype(BF16)
+    ends[0] = gain[...] * jnp.sum(part[0], axis=1)
+    ends[1] = jnp.sum(part[1], axis=1)
+    state[0, 0:poles, :] = ends[0].astype(BF16)
+    state[1, 0:poles, :] = ends[1].astype(BF16)
 
     def s_copy(o):
         other = lax.rem(ctx + o, n_ctx)
@@ -292,35 +303,65 @@
 
     lax.fori_loop(1, n_ctx, wait_state, 0)
 
-    def add_state(i, carried):
-        got = state_in[i].astype(F32)
-        return carried[0] + w_fwd[i] * got, carried[1] + w_bwd[i] * got
-
+    branch_row = lax.broadcasted_iota(jnp.int32, (SUB, chans), 0)
+    upper = branch_row < 4
+    tap_rows = [jnp.concatenate([taps[i], blank, taps[i], blank], axis=0) for i in range(3)]
+
+    def first_rows(i):
+        here = state_in[i, poles:, :].astype(F32)[0:SUB]
+        before = state_in[jnp.maximum(i - 1, 0), poles:, :].astype(F32)[SUB:]
+        before = jnp.where(i > 0, before, 0.0)
+        shifted = jnp.where(upper, pltpu.roll(before, 4, 0), pltpu.roll(here, 4, 0))
+        full = tap_rows[0] * here + tap_rows[1] * shifted + tap_rows[2] * before
+        return [(here[r + 3 : r + 4], full[r : r + 1], full[r + 1 : r + 2], full[r + 2 : r + 3]) for r in (0, 4)]
+
+    decay = jnp.exp(-rates)
+    gained = [gain[...] * jnp.exp(-rates * (rows - 1.0)), gain[...] * jnp.exp(-rates * (rows - 2.0))]
     none = jnp.zeros((poles, chans), F32)
-    before, after = lax.fori_loop(0, n_ctx, add_state, (none, none))
-    decayed = res[...] * jnp.exp(-rates)
-    part[0, :, 0, :] = decayed * before
-    part[1, :, 0, :] = decayed * gain[...] * after
-
-    def finish_rows(lo, n):
-        def add_fwd(p, acc):
-            return acc + fwd_pow[p, lo : lo + n, :] * part[0, p, 0:1, :]
-
-        def add_bwd(p, acc):
-            return acc + rev_pow[p, lo : lo + n, :] * part[1, p, 0:1, :]
-
-        whole = lax.fori_loop(0, poles, add_fwd, long_out[lo : lo + n, :])
-        gfp[0, lo : lo + n, :] = cot[...].astype(F32)[lo : lo + n] * whole
-        whole = lax.fori_loop(0, poles, add_bwd, grad_mix[lo : lo + n, :])
-        gfp[1, lo : lo + n, :] = whole * valp[lo : lo + n, :]
-        gfp[2, lo : lo + n, :] = whole * keyp[lo : lo + n, :]
-
-    finish_rows(0, SUB)
-    rim2 = remote(gfp.at[:, pl.ds(0, SUB), :], rim.at[1], rim_send.at[1], rim_recv.at[1], (prev_ctx, tp))
-    rim2.start()
-    finish_rows(SUB, rows - SUB)
-    rim2.wait()
-    gfp[:, rows : rows + SUB, :] = jnp.where(ctx < n_ctx - 1, rim[1], 0.0)
+
+    def add_before(i, total):
+        (_, _, k0, v0), (_, _, k1, v1) = first_rows(i)
+        end = state_in[i, 0:poles, :].astype(F32) + gained[0] * (k0 * v0) + gained[1] * (k1 * v1)
+        return total + w_fwd[i] * end
+
+    def add_after(i, total):
+        (c0, g0, _, _), (c1, g1, _, _) = first_rows(i)
+        return total + w_bwd[i] * (state_in[i, 0:poles, :].astype(F32) + c0 * g0 + decay * (c1 * g1))
+
+    before = lax.fori_loop(0, ctx, add_before, none)
+    after = lax.fori_loop(ctx + 1, n_ctx, add_after, none)
+    out_gain = res[...] * gain[...]
+    part[0, :, 0, :] = res[...] * decay * before
+    part[1, :, 0, :] = out_gain * decay * after
+
+    (c0, g0, k0, v0), (c1, g1, k1, v1) = first_rows(ctx)
+    keyp[0:1, :], valp[0:1, :], keyp[1:2, :], valp[1:2, :] = k0, v0, k1, v1
+    mix0, mix1, gl0, gl1 = k0 * v0, k1 * v1, c0 * g0, c1 * g1
+    taps0, taps1 = kern[0:1, :], kern[1:2, :]
+    grad_mix[0:1, :] += taps0 * gl0 + taps1 * gl1
+    grad_mix[1:2, :] += taps0 * gl1
+    leaving = jnp.exp(-rates * float(rows)) * before + ends[0] + gained[0] * mix0 + gained[1] * mix1
+    (c0, g0, k0, v0), (c1, g1, k1, v1) = first_rows(jnp.minimum(ctx + 1, n_ctx - 1))
+    leaving = res[...] * decay * leaving
+    out0 = jnp.sum(leaving, axis=0, keepdims=True) + taps0 * (k0 * v0)
+    out1 = jnp.sum(leaving * decay, axis=0, keepdims=True) + taps1 * (k0 * v0) + taps0 * (k1 * v1)
+    adj0 = jnp.sum(out_gain * after, axis=0, keepdims=True)
+    adj1 = jnp.sum(out_gain * jnp.exp(rates) * (after - c0 * g0), axis=0, keepdims=True)
+    for j, pair in enumerate(((c0 * out0, c1 * out1), (adj0 * v0, adj1 * v1), (adj0 * k0, adj1 * k1))):
+        for r in range(2):
+            gfp[j, rows + r : rows + r + 1, :] = jnp.where(ctx < n_ctx - 1, pair[r], 0.0)
+
+    def add_fwd(p, acc):
+        return acc + fwd_pow[p] * part[0, p, 0:1, :]
+
+    def add_bwd(p, acc):
+        return acc + rev_pow[p] * part[1, p, 0:1, :]
+
+    whole = lax.fori_loop(0, poles, add_fwd, long_out[...] + kern[...] * mix0 + kern_late[...] * mix1)
+    gfp[0, 0:rows, :] = cot[...].astype(F32) * whole
+    whole = lax.fori_loop(0, poles, add_bwd, grad_mix[...])
+    gfp[1, 0:rows, :] = whole * valp[...]
+    gfp[2, 0:rows, :] = whole * keyp[...]
     for j in range(3):
         acc = taps[0, j : j + 1, :] * gfp[j, 0:rows, :]
         acc += taps[1, j : j + 1, :] * gfp[j, 1 : rows + 1, :]
@@ -337,53 +378,67 @@
 
         return lax.fori_loop(0, 3, branch, jnp.zeros((rows, chans), F32))
 
-    def r_copy(k, s):
-        return remote(rs_out.at[k, s], rs_in.at[k, s], r_send.at[k, s], r_recv.at[k, s], (ctx, neighbour[streams[k][1]]))
-
-    order = (3, 2, 0, 1)
+    def r_copy(k, s, p):
+        c, d, hops = streams[k]
+        there = neighbour[d] if c == 0 else jnp.where(s == hops - 1, diagonal[d], neighbour[d])
+        at = (k, s, piece(p))
+        return remote(rs_out.at[at], rs_in.at[at], r_send.at[k, s, p], r_recv.at[k, s, p], (ctx, there))
+
+    swap = remote(x_out, x_in, r_send.at[4, 0, 0], r_recv.at[4, 0, 0], (ctx, partner))
+
+    def slot_of(k, s):
+        c, d, hops = streams[k]
+        return at_z(col if c == 0 else 1 - col, z + (hops - s) * d)
+
+    for k in range(4):
+        rs_out[k, 0] = partial_of(slot_of(k, 0)).astype(BF16)
+        for p in range(PIECES):
+            r_copy(k, 0, p).start()
+    x_out[...] = partial_of(partner).astype(BF16)
+    swap.start()
 
     def reduce_step(s, _):
-        for k in order:
-            c, d, hops = streams[k]
-            slot = at_z(col if c == 0 else 1 - col, z + (hops - s) * d)
+        for k, (_, _, hops) in enumerate(streams):
 
             @pl.when(s < hops)
-            def _(k=k, slot=slot):
-                rs_out[k, s] = partial_of(slot).astype(BF16)
-
-                @pl.when(s > 0)
-                def _():
-                    r_copy(k, s - 1).wait_recv()
-                    rs_out[k, s] = (rs_out[k, s].astype(F32) + rs_in[k, s - 1].astype(F32)).astype(BF16)
-
-                r_copy(k, s).start()
-
-        return 0
-
-    lax.fori_loop(0, far, reduce_step, 0)
-    long_out[...] = partial_of(partner)
-    for k in (2, 3):
-        r_copy(k, streams[k][2] - 1).wait_recv()
-        long_out[...] += rs_in[k, streams[k][2] - 1].astype(F32)
-    x_out[...] = long_out[...].astype(BF16)
-    swap = remote(x_out, x_in, r_send.at[4, 0], r_recv.at[4, 0], (ctx, partner))
-    swap.start()
+            def _(k=k):
+                ready[k] = partial_of(slot_of(k, s))
+
+        for p in range(PIECES):
+            for k, (_, _, hops) in enumerate(streams):
+
+                @pl.when(s < hops)
+                def _(k=k, p=p):
+                    at = piece(p)
+                    r_copy(k, s - 1, p).wait_recv()
+                    rs_out[k, s, at] = (ready[k, at] + rs_in[k, s - 1, at].astype(F32)).astype(BF16)
+                    r_copy(k, s, p).start()
+
+        return 0
+
+    lax.fori_loop(1, far, reduce_step, 0)
     long_out[...] = partial_of(tp)
-    for k in (0, 1):
-        r_copy(k, streams[k][2] - 1).wait_recv()
-        long_out[...] += rs_in[k, streams[k][2] - 1].astype(F32)
     swap.wait_recv()
-    result[...] = (long_out[...] + x_in[...].astype(F32)).astype(BF16)
+    long_out[...] += x_in[...].astype(F32)
+    for p in range(PIECES):
+        at = piece(p)
+        for k, (_, _, hops) in enumerate(streams):
+            r_copy(k, hops - 1, p).wait_recv()
+        total = long_out[at]
+        for k, (_, _, hops) in enumerate(streams):
+            total += rs_in[k, hops - 1, at].astype(F32)
+        result[at] = total.astype(BF16)
     done = pltpu.make_async_copy(result, out_hbm, local_sem.at[0])
     done.start()
 
     swap.wait_send()
-    x_pair(tp, x_hbm).wait_send()
+    x_pair(tp).wait_send()
     for k, (c, d, hops) in enumerate(streams):
 
         def left(s, _, k=k):
-            g_copy(k, s, tp).wait_send()
-            r_copy(k, s - 1).wait_send()
+            for p in range(PIECES):
+                g_copy(k, s, p, tp).wait_send()
+                r_copy(k, s - 1, p).wait_send()
             return 0
 
         lax.fori_loop(1, hops + 1, left, 0)
@@ -413,19 +468,21 @@
         vmem((poles, rows, chans), F32),
         vmem((poles, rows, chans), F32),
         vmem((rows, chans), F32),
+        vmem((rows, chans), F32),
         vmem((rows, SUB, chans), F32),
         vmem((poles, chans), F32),
         vmem((n_ctx, poles, chans), F32),
         vmem((n_ctx, poles, chans), F32),
         vmem((2, poles, SUB, chans), F32),
-        vmem((2, poles, chans), BF16),
-        vmem((n_ctx, poles, chans), BF16),
-        vmem((2, 3, SUB, chans), F32),
+        vmem((2, poles, chans), F32),
+        vmem((2, poles + 2 * SUB, chans), BF16),
+        vmem((n_ctx, poles + 2 * SUB, chans), BF16),
         vmem((3, rows + SUB, chans), F32),
         vmem((2, SUB, rows, chans), F32),
         vmem((rows, chans), F32),
         vmem((rows, chans), F32),
         vmem((3, rows, chans), BF16),
+        vmem((4, rows, chans), F32),
         vmem((4, far, rows, chans), BF16),
         vmem((4, far, rows, chans), BF16),
         vmem((rows, chans), BF16),
@@ -433,14 +490,12 @@
         vmem((rows, chans), BF16),
         dma((5,)),
         dma((3,)),
-        dma((5, far + 1)),
-        dma((5, far + 1)),
+        dma((5, far + 1, PIECES)),
+        dma((5, far + 1, PIECES)),
         dma((n_ctx,)),
         dma((n_ctx,)),
-        dma((2,)),
-        dma((2,)),
-        dma((5, far)),
-        dma((5, far)),
+        dma((5, far, PIECES)),
+        dma((5, far, PIECES)),
     ]
     return pl.pallas_call(
         functools.partial(kernel, n_ctx, n_tp),

time: 60.6 us -> 57.1 us (0.942)
  Pallas kernels: 58.4 us -> 55 us
    pallas_call x1, Pallas kernels: 58.4 us -> 55 us  [body(): pl.pallas_call(functools.partial(kernel, n_ctx, n_tp), out_shape=jax.Shap...]
where the time goes in v2:
time: 57.1 us; the launch traced here: 56.5 us
  Pallas kernels  55 us (96%)
  local copies, waits for them, and re-layouts  1.47 us (3%)
    pallas_call x1, Pallas kernels, body(): pl.pallas_call(functools.partial(kernel, n_ctx, n_tp), out_shape=jax.Shap...  55 us
    unnamed x1, local copies, waits for them, and re-layouts  1.47 us

profile of v2, /device:TPU:8, one launch (start us, length us, event | category | flops | bytes accessed | tf_op | source)
XLA Modules:
  0.0 56.5 jit_solution(8077249950133758647)
XLA Ops:
  0.0 55.0 %hyena_input_grad.1 = bf16[128,256]{1,0:T(8,128)(2,1)} custom-call(bf16[128,256]{1,0:T(8,128)(2,1)} %x_hbm.1, bf16[3,4096,256]{2,1,0:T(8,128)(2,1)} %bitcast.3, f32[3,3,256]{2,1,0:T(4,128)} %taps_hbm.1, f32[16,256]{1,0:T(8,128)} %bitcast.4, f32[16,256]{1,0:T(8,128)} %bitcast.5, bf16[128,256]{1,0:T(8,128)(2,1)} %cot_hbm.1), custom_call_target="tpu_custom_call" | custom-call | flops 1610612736 | bytes 6291456 | tf_op jit(solution)/shard_map/hyena_input_grad/pallas_call | solution.py:500
  55.0 1.5 %copy.8 = bf16[128,256]{1,0:T(8,128)(2,1)} copy(bf16[128,256]{1,0:T(8,128)(2,1)} %hyena_input_grad.1) | data formatting | bytes 131072

commit v3 on v2

--- a/solution.py
+++ b/solution.py
@@ -74,14 +74,15 @@
     g_recv,
     s_send,
     s_recv,
+    met,
     r_send,
     r_recv,
 ):
     rows, chans = x_hbm.shape
     poles = rate_hbm.shape[0]
     ring = n_tp // COLUMNS
-    far, near = (ring - 1 + 1) // 2, (ring - 1) // 2
-    streams = ((0, 1, far), (0, -1, near), (1, 1, near), (1, -1, far))
+    hops = ring // 2 - 1
+    streams = ((0, 1), (1, -1), (0, -1), (1, 1))
     ctx = lax.axis_index("ctx")
     tp = lax.axis_index("tp")
     col, z = tp // ring, tp % ring
@@ -89,19 +90,32 @@
     def at_z(column, zz):
         return column * ring + (zz + 2 * ring) % ring
 
+    def column_of(c):
+        return col if c == 0 else 1 - col
+
     partner = at_z(1 - col, z)
-    neighbour = {1: at_z(col, z + 1), -1: at_z(col, z - 1)}
-    diagonal = {1: at_z(1 - col, z + 1), -1: at_z(1 - col, z - 1)}
+
+    rounds = n_ctx.bit_length() - 1
+
+    def across(r):
+        bit = (ctx // 2**r) % 2
+        return ctx + 2**r * (1 - 2 * bit)
 
     barrier = pltpu.get_barrier_semaphore()
-    for other in (neighbour[1], neighbour[-1], diagonal[1], diagonal[-1], partner):
+    others = [at_z(col, z + d) for d in (1, -1, 2, -2)]
+    others += [at_z(1 - col, z + d) for d in ((1, -1) if hops > 1 else (1, -1, 2, -2))] + [partner]
+    for other in others:
         pl.semaphore_signal(barrier, inc=1, device_id=(ctx, other), device_id_type=MESH)
-
-    def greet(o, _):
-        pl.semaphore_signal(barrier, inc=1, device_id=(lax.rem(ctx + o, n_ctx), tp), device_id_type=MESH)
-        return 0
-
-    lax.fori_loop(1, n_ctx, greet, 0)
+    for r in range(rounds):
+        pl.semaphore_signal(barrier, inc=1, device_id=(across(r), tp), device_id_type=MESH)
+
+    def greet(r):
+        if r < rounds:
+            pl.semaphore_signal(met.at[r], inc=1, device_id=(across(r), tp), device_id_type=MESH)
+
+    def greeted(r):
+        if r < rounds:
+            pl.semaphore_wait(met.at[r], 1)
 
     w_copies = [pltpu.make_async_copy(w_hbm.at[j], w.at[j], w_sem.at[j]) for j in range(3)]
     small = [
@@ -112,7 +126,7 @@
     ]
     for c in small + w_copies:
         c.start()
-    pl.semaphore_wait(barrier, 5 + n_ctx - 1)
+    pl.semaphore_wait(barrier, len(others) + rounds)
 
     def remote(src, dst, send, recv, device):
         return pltpu.make_async_remote_copy(
@@ -124,20 +138,39 @@
     def piece(p):
         return pl.ds(p * size, size)
 
-    def g_copy(k, s, p, slot, src=None):
-        c, d, _ = streams[k]
-        here = xg.at[slot, piece(p)]
-        there = neighbour[d] if src is None or c == 0 else diagonal[d]
-        src = here if src is None else src.at[piece(p)]
-        return remote(src, here, g_send.at[k, s, p], g_recv.at[k, s, p], (ctx, there))
-
-    def x_pair(slot):
-        return remote(x_hbm, xg.at[slot], g_send.at[4, 0, 0], g_recv.at[4, 0, 0], (ctx, partner))
-
-    for p in range(PIECES):
+    def halves(k):
+        return (0, 1) if streams[k][1] > 0 else (1, 0)
+
+    def g_copy(k, s, p):
+        c, d = streams[k]
+        skip = 2 if s > hops else 1
+        held = z - (s - skip) * d
+        own = s == skip
+        slot = tp if own else at_z(column_of(c), held)
+        there = at_z(1 - col if own and c == 1 else col, z + skip * d)
+        src = x_hbm.at[piece(p)] if own else xg.at[slot, piece(p)]
+        return remote(src, xg.at[slot, piece(p)], g_send.at[k, s, p], g_recv.at[k, s, p], (ctx, there))
+
+    def arrived(k, s, p):
+        here = xg.at[at_z(column_of(streams[k][0]), z - s * streams[k][1]), piece(p)]
+        remote(here, here, g_send.at[k, s, p], g_recv.at[k, s, p], (ctx, partner)).wait_recv()
+
+    x_pair = remote(x_hbm, xg.at[tp], g_send.at[4, 0, 0], g_recv.at[4, 0, 0], (ctx, partner))
+
+    def forward(s, i):
         for k in range(4):
-            g_copy(k, 1, p, tp, x_hbm).start()
-    x_pair(tp).start()
+            p = halves(k)[i]
+            if s > 0:
+                arrived(k, s, p)
+            if s == hops - 1 and i == 0:
+                g_copy(k, hops + 1, p).start()
+            if s < hops:
+                g_copy(k, s + 1, p).start()
+
+    for i in range(PIECES):
+        forward(0, i)
+    x_pair.start()
+    greet(0)
 
     for c in small[1:]:
         c.wait()
@@ -163,53 +196,35 @@
         w_bwd[i] = jnp.where(i > ctx, weight, 0.0)
         return 0
 
-    def project(slot):
-        block = xg[slot]
-        start = pl.multiple_of(slot * chans, chans)
-
-        def branch(j, _):
-            proj[j, SUB:, :] += jnp.dot(block, w[j, pl.ds(start, chans), :], preferred_element_type=F32)
-            return 0
-
-        lax.fori_loop(0, 3, branch, 0)
+    def project(slots):
+        for j in range(3):
+            total = proj[j, SUB:, :]
+            for slot in slots:
+                start = pl.multiple_of(slot * chans, chans)
+                total += jnp.dot(xg[slot], w[j, pl.ds(start, chans), :], preferred_element_type=F32)
+            proj[j, SUB:, :] = total
 
     proj[...] = jnp.zeros_like(proj)
     small[0].wait()
     for c in w_copies:
         c.wait()
-    project(tp)
-    per_step = -(-poles // far)
-    ctx_per_step = -(-n_ctx // far)
-
-    def gather_step(s, _):
-        slots = [at_z(col if c == 0 else 1 - col, z - s * d) for c, d, _ in streams]
-        for p in range(PIECES):
-            for k, (_, _, hops) in enumerate(streams):
-
-                @pl.when(s <= hops)
-                def _(k=k, p=p, hops=hops):
-                    g_copy(k, s, p, slots[k]).wait_recv()
-
-                    @pl.when(s < hops)
-                    def _():
-                        g_copy(k, s + 1, p, slots[k]).start()
-
-        for k, (_, _, hops) in enumerate(streams):
-
-            @pl.when(s <= hops)
-            def _(k=k):
-                project(slots[k])
-
-        @pl.when(s == min(2, far))
-        def _():
-            x_pair(partner).wait_recv()
-            project(partner)
-
-        lax.fori_loop((s - 1) * per_step, jnp.minimum(s * per_step, poles), tables, 0)
-        lax.fori_loop((s - 1) * ctx_per_step, jnp.minimum(s * ctx_per_step, n_ctx), state_weights, 0)
-        return 0
-
-    lax.fori_loop(1, far + 1, gather_step, 0)
+    project([tp])
+    per_step = -(-poles // hops)
+    ctx_per_step = -(-n_ctx // hops)
+    for s in range(1, hops + 1):
+        for i in range(PIECES):
+            forward(s, i)
+        project([at_z(column_of(c), z - s * d) for c, d in streams])
+        greeted(s - 1)
+        greet(s)
+        lax.fori_loop((s - 1) * per_step, min(s * per_step, poles), tables, 0)
+        lax.fori_loop((s - 1) * ctx_per_step, min(s * ctx_per_step, n_ctx), state_weights, 0)
+        if s == 1:
+            x_pair.wait_recv()
+            project([partner])
+    for k in range(4):
+        arrived(k, hops + 1, halves(k)[0])
+    project([at_z(col, z + hops + 1), at_z(1 - col, z + hops + 1)])
 
     def spread_rows(i, _):
         block = kern[pl.ds(pl.multiple_of(SUB * i, SUB), SUB), :]
@@ -257,6 +272,11 @@
     ends[1] = jnp.sum(part[1], axis=1)
     state[0, 0:poles, :] = ends[0].astype(BF16)
     state[1, 0:poles, :] = ends[1].astype(BF16)
+
+    greeted(hops)
+    for r in range(hops + 1, rounds):
+        greet(r)
+        greeted(r)
 
     def s_copy(o):
         other = lax.rem(ctx + o, n_ctx)
@@ -370,78 +390,91 @@
 
     def partial_of(slot):
         start = pl.multiple_of(slot * chans, chans)
-
-        def branch(j, acc):
-            return acc + lax.dot_general(
+        total = jnp.zeros((rows, chans), F32)
+        for j in range(3):
+            total += lax.dot_general(
                 gp[j], w[j, pl.ds(start, chans), :], (((1,), (1,)), ((), ())), preferred_element_type=F32
             )
-
-        return lax.fori_loop(0, 3, branch, jnp.zeros((rows, chans), F32))
+        return total
+
+    def block_at(k, distance):
+        c, d = streams[k]
+        return at_z(column_of(c), z + distance * d)
 
     def r_copy(k, s, p):
-        c, d, hops = streams[k]
-        there = neighbour[d] if c == 0 else jnp.where(s == hops - 1, diagonal[d], neighbour[d])
+        c, d = streams[k]
+        there = at_z(1 - col if c == 1 and s == hops else col, z + d)
         at = (k, s, piece(p))
         return remote(rs_out.at[at], rs_in.at[at], r_send.at[k, s, p], r_recv.at[k, s, p], (ctx, there))
 
+    def opposite(k):
+        c, d = streams[k]
+        p = halves(k)[0]
+        there = at_z(1 - col if c == 1 and hops == 1 else col, z + 2 * d)
+        at = (k, 0, piece(p))
+        return remote(rs_out.at[at], rs_in.at[at], r_send.at[k, 0, p], r_recv.at[k, 0, p], (ctx, there))
+
     swap = remote(x_out, x_in, r_send.at[4, 0, 0], r_recv.at[4, 0, 0], (ctx, partner))
 
-    def slot_of(k, s):
-        c, d, hops = streams[k]
-        return at_z(col if c == 0 else 1 - col, z + (hops - s) * d)
-
-    for k in range(4):
-        rs_out[k, 0] = partial_of(slot_of(k, 0)).astype(BF16)
-        for p in range(PIECES):
-            r_copy(k, 0, p).start()
+    for c in range(COLUMNS):
+        both = partial_of(at_z(column_of(c), z + hops + 1)).astype(BF16)
+        for k in range(4):
+            if streams[k][0] == c:
+                at = piece(halves(k)[0])
+                rs_out[k, 0, at] = both[halves(k)[0] * size : halves(k)[0] * size + size]
+                opposite(k).start()
+    for pair in ((0, 1), (2, 3)):
+        for k in pair:
+            rs_out[k, 1] = partial_of(block_at(k, hops)).astype(BF16)
+        for i in range(PIECES):
+            for k in pair:
+                r_copy(k, 1, halves(k)[i]).start()
     x_out[...] = partial_of(partner).astype(BF16)
     swap.start()
 
-    def reduce_step(s, _):
-        for k, (_, _, hops) in enumerate(streams):
-
-            @pl.when(s < hops)
-            def _(k=k):
-                ready[k] = partial_of(slot_of(k, s))
-
-        for p in range(PIECES):
-            for k, (_, _, hops) in enumerate(streams):
-
-                @pl.when(s < hops)
-                def _(k=k, p=p):
-                    at = piece(p)
-                    r_copy(k, s - 1, p).wait_recv()
-                    rs_out[k, s, at] = (ready[k, at] + rs_in[k, s - 1, at].astype(F32)).astype(BF16)
-                    r_copy(k, s, p).start()
-
-        return 0
-
-    lax.fori_loop(1, far, reduce_step, 0)
+    for s in range(2, hops + 1):
+        for k in range(4):
+            ready[k] = partial_of(block_at(k, hops + 1 - s))
+        for i in range(PIECES):
+            for k in range(4):
+                p = halves(k)[i]
+                at = piece(p)
+                total = ready[k, at]
+                if s == 2 and i == 0:
+                    opposite(k).wait_recv()
+                    total += rs_in[k, 0, at].astype(F32)
+                r_copy(k, s - 1, p).wait_recv()
+                rs_out[k, s, at] = (total + rs_in[k, s - 1, at].astype(F32)).astype(BF16)
+                r_copy(k, s, p).start()
+
     long_out[...] = partial_of(tp)
     swap.wait_recv()
     long_out[...] += x_in[...].astype(F32)
+    if hops == 1:
+        for k in range(4):
+            at = piece(halves(k)[0])
+            opposite(k).wait_recv()
+            long_out[at] += rs_in[k, 0, at].astype(F32)
     for p in range(PIECES):
         at = piece(p)
-        for k, (_, _, hops) in enumerate(streams):
-            r_copy(k, hops - 1, p).wait_recv()
+        for k in range(4):
+            r_copy(k, hops, p).wait_recv()
         total = long_out[at]
-        for k, (_, _, hops) in enumerate(streams):
-            total += rs_in[k, hops - 1, at].astype(F32)
+        for k in range(4):
+            total += rs_in[k, hops, at].astype(F32)
         result[at] = total.astype(BF16)
     done = pltpu.make_async_copy(result, out_hbm, local_sem.at[0])
     done.start()
 
     swap.wait_send()
-    x_pair(tp).wait_send()
-    for k, (c, d, hops) in enumerate(streams):
-
-        def left(s, _, k=k):
-            for p in range(PIECES):
-                g_copy(k, s, p, tp).wait_send()
-                r_copy(k, s - 1, p).wait_send()
-            return 0
-
-        lax.fori_loop(1, hops + 1, left, 0)
+    x_pair.wait_send()
+    for k in range(4):
+        g_copy(k, hops + 1, halves(k)[0]).wait_send()
+        opposite(k).wait_send()
+        for p in range(PIECES):
+            for s in range(1, hops + 1):
+                g_copy(k, s, p).wait_send()
+                r_copy(k, s, p).wait_send()
     done.wait()
 
 
@@ -449,7 +482,7 @@
     rows, chans = inputs.shape
     width = w_in.shape[0]
     poles = pole_rates.shape[1]
-    far = n_tp // COLUMNS // 2
+    steps = n_tp // COLUMNS // 2 + 1
     vmem = pltpu.VMEM
     dma = pltpu.SemaphoreType.DMA
     scratch = [
@@ -483,19 +516,20 @@
         vmem((rows, chans), F32),
         vmem((3, rows, chans), BF16),
         vmem((4, rows, chans), F32),
-        vmem((4, far, rows, chans), BF16),
-        vmem((4, far, rows, chans), BF16),
+        vmem((4, steps - 1, rows, chans), BF16),
+        vmem((4, steps - 1, rows, chans), BF16),
         vmem((rows, chans), BF16),
         vmem((rows, chans), BF16),
         vmem((rows, chans), BF16),
         dma((5,)),
         dma((3,)),
-        dma((5, far + 1, PIECES)),
-        dma((5, far + 1, PIECES)),
+        dma((5, steps, PIECES)),
+        dma((5, steps, PIECES)),
         dma((n_ctx,)),
         dma((n_ctx,)),
-        dma((5, far, PIECES)),
-        dma((5, far, PIECES)),
+        pltpu.SemaphoreType.REGULAR((n_ctx.bit_length(),)),
+        dma((5, steps - 1, PIECES)),
+        dma((5, steps - 1, PIECES)),
     ]
     return pl.pallas_call(
         functools.partial(kernel, n_ctx, n_tp),

time: 57.1 us -> 53.1 us (0.930)
  Pallas kernels: 55 us -> 51.3 us
    pallas_call x1, Pallas kernels: 55 us -> 51.3 us  [body(): pl.pallas_call(functools.partial(kernel, n_ctx, n_tp), out_shape=jax.Shap...]
where the time goes in v3:
time: 53.1 us; the launch traced here: 52.8 us
  Pallas kernels  51.3 us (97%)
  local copies, waits for them, and re-layouts  1.47 us (3%)
    pallas_call x1, Pallas kernels, body(): pl.pallas_call(functools.partial(kernel, n_ctx, n_tp), out_shape=jax.Shap...  51.3 us
    unnamed x1, local copies, waits for them, and re-layouts  1.47 us

profile of v3, /device:TPU:8, one launch (start us, length us, event | category | flops | bytes accessed | tf_op | source)
XLA Modules:
  0.0 52.8 jit_solution(9690772706581222217)
XLA Ops:
  0.0 51.3 %hyena_input_grad.1 = bf16[128,256]{1,0:T(8,128)(2,1)} custom-call(bf16[128,256]{1,0:T(8,128)(2,1)} %x_hbm.1, bf16[3,4096,256]{2,1,0:T(8,128)(2,1)} %bitcast.3, f32[3,3,256]{2,1,0:T(4,128)} %taps_hbm.1, f32[16,256]{1,0:T(8,128)} %bitcast.4, f32[16,256]{1,0:T(8,128)} %bitcast.5, bf16[128,256]{1,0:T(8,128)(2,1)} %cot_hbm.1), custom_call_target="tpu_custom_call" | custom-call | flops 1610612736 | bytes 6291456 | tf_op jit(solution)/shard_map/hyena_input_grad/pallas_call | solution.py:534
  51.3 1.5 %copy.8 = bf16[128,256]{1,0:T(8,128)(2,1)} copy(bf16[128,256]{1,0:T(8,128)(2,1)} %hyena_input_grad.1) | data formatting | bytes 131072

commit v4 on v3

--- a/solution.py
+++ b/solution.py
@@ -82,7 +82,8 @@
     poles = rate_hbm.shape[0]
     ring = n_tp // COLUMNS
     hops = ring // 2 - 1
-    streams = ((0, 1), (1, -1), (0, -1), (1, 1))
+    streams = ((0, 1), (0, -1), (1, 1), (1, -1))
+    mine, theirs = (0, 1), (2, 3)
     ctx = lax.axis_index("ctx")
     tp = lax.axis_index("tp")
     col, z = tp // ring, tp % ring
@@ -103,7 +104,7 @@
 
     barrier = pltpu.get_barrier_semaphore()
     others = [at_z(col, z + d) for d in (1, -1, 2, -2)]
-    others += [at_z(1 - col, z + d) for d in ((1, -1) if hops > 1 else (1, -1, 2, -2))] + [partner]
+    others += [at_z(1 - col, z + d) for d in (1, -1)] + [partner]
     for other in others:
         pl.semaphore_signal(barrier, inc=1, device_id=(ctx, other), device_id_type=MESH)
     for r in range(rounds):
@@ -144,12 +145,14 @@
     def g_copy(k, s, p):
         c, d = streams[k]
         skip = 2 if s > hops else 1
-        held = z - (s - skip) * d
-        own = s == skip
-        slot = tp if own else at_z(column_of(c), held)
-        there = at_z(1 - col if own and c == 1 else col, z + skip * d)
-        src = x_hbm.at[piece(p)] if own else xg.at[slot, piece(p)]
-        return remote(src, xg.at[slot, piece(p)], g_send.at[k, s, p], g_recv.at[k, s, p], (ctx, there))
+        held, there = at_z(column_of(c), z - (s - skip) * d), at_z(col, z + skip * d)
+        if c == 1 and s == 1:
+            held, there = at_z(col, z - d), partner
+        if c == 1 and s == 2:
+            held, there = at_z(col, z - d), at_z(1 - col, z + d)
+        block = xg.at[held, piece(p)]
+        src = x_hbm.at[piece(p)] if c == 0 and s == 1 else block
+        return remote(src, block, g_send.at[k, s, p], g_recv.at[k, s, p], (ctx, there))
 
     def arrived(k, s, p):
         here = xg.at[at_z(column_of(streams[k][0]), z - s * streams[k][1]), piece(p)]
@@ -157,18 +160,21 @@
 
     x_pair = remote(x_hbm, xg.at[tp], g_send.at[4, 0, 0], g_recv.at[4, 0, 0], (ctx, partner))
 
-    def forward(s, i):
-        for k in range(4):
-            p = halves(k)[i]
-            if s > 0:
-                arrived(k, s, p)
-            if s == hops - 1 and i == 0:
-                g_copy(k, hops + 1, p).start()
-            if s < hops:
-                g_copy(k, s + 1, p).start()
+    def forward(k, s, i):
+        p = halves(k)[i]
+        arrived(k, s, p)
+        if s == hops - 1 and i == 0:
+            g_copy(k, hops + 1, p).start()
+        if s < hops:
+            g_copy(k, s + 1, p).start()
+
+    def block_at(k, distance):
+        c, d = streams[k]
+        return at_z(column_of(c), z + distance * d)
 
     for i in range(PIECES):
-        forward(0, i)
+        for k in mine:
+            g_copy(k, 1, halves(k)[i]).start()
     x_pair.start()
     greet(0)
 
@@ -211,20 +217,45 @@
     project([tp])
     per_step = -(-poles // hops)
     ctx_per_step = -(-n_ctx // hops)
-    for s in range(1, hops + 1):
-        for i in range(PIECES):
-            forward(s, i)
-        project([at_z(column_of(c), z - s * d) for c, d in streams])
+
+    def beside(s):
         greeted(s - 1)
         greet(s)
         lax.fori_loop((s - 1) * per_step, min(s * per_step, poles), tables, 0)
         lax.fori_loop((s - 1) * ctx_per_step, min(s * ctx_per_step, n_ctx), state_weights, 0)
-        if s == 1:
-            x_pair.wait_recv()
-            project([partner])
+
+    for i in range(PIECES):
+        for k in mine:
+            forward(k, 1, i)
+            g_copy(k + 2, 2, halves(k)[i]).start()
+    for i in range(PIECES):
+        for k in theirs:
+            g_copy(k, 1, halves(k)[i]).start()
+    project([block_at(k, -1) for k in mine])
+    beside(1)
+    for s in range(2, hops):
+        for group in (mine, theirs):
+            for i in range(PIECES):
+                for k in group:
+                    forward(k, s, i)
+        project([block_at(k, -s) for k in range(4)])
+        beside(s)
+    x_pair.wait_recv()
+    for k in mine:
+        for i in range(PIECES):
+            forward(k, hops, i)
+    project([block_at(k, -hops) for k in mine] + [partner])
+    beside(hops)
+    for k in theirs:
+        for i in range(PIECES):
+            arrived(k, 1, halves(k)[i])
+    project([block_at(k, -1) for k in theirs])
+    for k in theirs:
+        for i in range(PIECES):
+            forward(k, hops, i)
     for k in range(4):
         arrived(k, hops + 1, halves(k)[0])
-    project([at_z(col, z + hops + 1), at_z(1 - col, z + hops + 1)])
+    project([block_at(k, -hops) for k in theirs] + [block_at(0, hops + 1), block_at(2, hops + 1)])
 
     def spread_rows(i, _):
         block = kern[pl.ds(pl.multiple_of(SUB * i, SUB), SUB), :]
@@ -279,15 +310,15 @@
         greeted(r)
 
     def s_copy(o):
-        other = lax.rem(ctx + o, n_ctx)
+        other = ctx
+        for r in range(rounds):
+            if o >> r & 1:
+                other = other + across(r) - ctx
         which = (other < ctx).astype(jnp.int32)
         return remote(state.at[which], state_in.at[ctx], s_send.at[o], s_recv.at[o], (other, tp))
 
-    def send_state(o, _):
+    for o in range(n_ctx - 1, 0, -1):
         s_copy(o).start()
-        return 0
-
-    lax.fori_loop(1, n_ctx, send_state, 0)
 
     tiles = rows // SUB
 
@@ -317,11 +348,8 @@
     local_conv(0, True, long_out)
     local_conv(1, False, grad_mix)
 
-    def wait_state(o, _):
+    for o in range(1, n_ctx):
         s_copy(o).wait()
-        return 0
-
-    lax.fori_loop(1, n_ctx, wait_state, 0)
 
     branch_row = lax.broadcasted_iota(jnp.int32, (SUB, chans), 0)
     upper = branch_row < 4
@@ -397,70 +425,76 @@
             )
         return total
 
-    def block_at(k, distance):
-        c, d = streams[k]
-        return at_z(column_of(c), z + distance * d)
-
     def r_copy(k, s, p):
         c, d = streams[k]
-        there = at_z(1 - col if c == 1 and s == hops else col, z + d)
+        there = at_z(col, z + d)
+        if c == 1 and s == hops - 1:
+            there = at_z(1 - col, z + d)
+        if c == 1 and s == hops:
+            there = partner
         at = (k, s, piece(p))
         return remote(rs_out.at[at], rs_in.at[at], r_send.at[k, s, p], r_recv.at[k, s, p], (ctx, there))
 
     def opposite(k):
-        c, d = streams[k]
         p = halves(k)[0]
-        there = at_z(1 - col if c == 1 and hops == 1 else col, z + 2 * d)
         at = (k, 0, piece(p))
+        there = at_z(col, z + 2 * streams[k][1])
         return remote(rs_out.at[at], rs_in.at[at], r_send.at[k, 0, p], r_recv.at[k, 0, p], (ctx, there))
 
     swap = remote(x_out, x_in, r_send.at[4, 0, 0], r_recv.at[4, 0, 0], (ctx, partner))
 
-    for c in range(COLUMNS):
-        both = partial_of(at_z(column_of(c), z + hops + 1)).astype(BF16)
-        for k in range(4):
-            if streams[k][0] == c:
-                at = piece(halves(k)[0])
-                rs_out[k, 0, at] = both[halves(k)[0] * size : halves(k)[0] * size + size]
-                opposite(k).start()
-    for pair in ((0, 1), (2, 3)):
-        for k in pair:
-            rs_out[k, 1] = partial_of(block_at(k, hops)).astype(BF16)
+    for group in (mine, theirs):
+        both = partial_of(block_at(group[0], hops + 1)).astype(BF16)
+        for k in group:
+            p = halves(k)[0]
+            rs_out[k, 0, piece(p)] = both[p * size : p * size + size]
+            opposite(k).start()
+    for group, s, distance in ((theirs, 1, hops), (mine, 1, hops), (theirs, hops, 1)):
+        for k in group:
+            rs_out[k, s] = partial_of(block_at(k, distance)).astype(BF16)
         for i in range(PIECES):
-            for k in pair:
-                r_copy(k, 1, halves(k)[i]).start()
+            for k in group:
+                r_copy(k, s, halves(k)[i]).start()
     x_out[...] = partial_of(partner).astype(BF16)
     swap.start()
 
-    for s in range(2, hops + 1):
+    for s in range(2, hops):
         for k in range(4):
             ready[k] = partial_of(block_at(k, hops + 1 - s))
-        for i in range(PIECES):
-            for k in range(4):
-                p = halves(k)[i]
-                at = piece(p)
-                total = ready[k, at]
-                if s == 2 and i == 0:
-                    opposite(k).wait_recv()
-                    total += rs_in[k, 0, at].astype(F32)
-                r_copy(k, s - 1, p).wait_recv()
-                rs_out[k, s, at] = (total + rs_in[k, s - 1, at].astype(F32)).astype(BF16)
-                r_copy(k, s, p).start()
+        for group in (theirs, mine):
+            for i in range(PIECES):
+                for k in group:
+                    p = halves(k)[i]
+                    at = piece(p)
+                    total = ready[k, at]
+                    if s == 2 and i == 0:
+                        opposite(k).wait_recv()
+                        total += rs_in[k, 0, at].astype(F32)
+                    r_copy(k, s - 1, p).wait_recv()
+                    rs_out[k, s, at] = (total + rs_in[k, s - 1, at].astype(F32)).astype(BF16)
+                    r_copy(k, s, p).start()
+
+    for k in mine:
+        ready[k] = partial_of(block_at(k, 1))
+    for i in range(PIECES):
+        for k in mine:
+            p = halves(k)[i]
+            at = piece(p)
+            total = ready[k, at]
+            for other, step in ((k + 2, hops), (k, hops - 1), (k + 2, hops - 1)):
+                r_copy(other, step, p).wait_recv()
+                total += rs_in[other, step, at].astype(F32)
+            rs_out[k, hops, at] = total.astype(BF16)
+            r_copy(k, hops, p).start()
 
     long_out[...] = partial_of(tp)
     swap.wait_recv()
     long_out[...] += x_in[...].astype(F32)
-    if hops == 1:
-        for k in range(4):
-            at = piece(halves(k)[0])
-            opposite(k).wait_recv()
-            long_out[at] += rs_in[k, 0, at].astype(F32)
     for p in range(PIECES):
         at = piece(p)
-        for k in range(4):
+        total = long_out[at]
+        for k in mine:
             r_copy(k, hops, p).wait_recv()
-        total = long_out[at]
-        for k in range(4):
             total += rs_in[k, hops, at].astype(F32)
         result[at] = total.astype(BF16)
     done = pltpu.make_async_copy(result, out_hbm, local_sem.at[0])

time: 53.1 us -> 49.2 us (0.927)
  Pallas kernels: 51.3 us -> 47.5 us
    pallas_call x1, Pallas kernels: 51.3 us -> 47.5 us  [body(): pl.pallas_call(functools.partial(kernel, n_ctx, n_tp), out_shape=jax.Shap...]
where the time goes in v4:
time: 49.2 us; the launch traced here: 49 us
  Pallas kernels  47.5 us (97%)
  local copies, waits for them, and re-layouts  1.47 us (3%)
    pallas_call x1, Pallas kernels, body(): pl.pallas_call(functools.partial(kernel, n_ctx, n_tp), out_shape=jax.Shap...  47.5 us
    unnamed x1, local copies, waits for them, and re-layouts  1.47 us

profile of v4, /device:TPU:8, one launch (start us, length us, event | category | flops | bytes accessed | tf_op | source)
XLA Modules:
  0.0 49.0 jit_solution(9180503514766947726)
XLA Ops:
  0.0 47.5 %hyena_input_grad.1 = bf16[128,256]{1,0:T(8,128)(2,1)} custom-call(bf16[128,256]{1,0:T(8,128)(2,1)} %x_hbm.1, bf16[3,4096,256]{2,1,0:T(8,128)(2,1)} %bitcast.3, f32[3,3,256]{2,1,0:T(4,128)} %taps_hbm.1, f32[16,256]{1,0:T(8,128)} %bitcast.4, f32[16,256]{1,0:T(8,128)} %bitcast.5, bf16[128,256]{1,0:T(8,128)(2,1)} %cot_hbm.1), custom_call_target="tpu_custom_call" | custom-call | flops 1610612736 | bytes 6291456 | tf_op jit(solution)/shard_map/hyena_input_grad/pallas_call | solution.py:568
  47.5 1.5 %copy.8 = bf16[128,256]{1,0:T(8,128)(2,1)} copy(bf16[128,256]{1,0:T(8,128)(2,1)} %hyena_input_grad.1) | data formatting | bytes 131072

commit v5 on v4

--- a/solution.py
+++ b/solution.py
@@ -32,7 +32,7 @@
     rate_hbm,
     res_hbm,
     cot_hbm,
-    out_hbm,
+    out,
     w,
     xg,
     taps,
@@ -67,7 +67,8 @@
     rs_in,
     x_out,
     x_in,
-    result,
+    far_out,
+    far_in,
     local_sem,
     w_sem,
     g_send,
@@ -103,7 +104,7 @@
         return ctx + 2**r * (1 - 2 * bit)
 
     barrier = pltpu.get_barrier_semaphore()
-    others = [at_z(col, z + d) for d in (1, -1, 2, -2)]
+    others = [at_z(col, z + d) for d in (1, -1, 2, -2, hops + 1)]
     others += [at_z(1 - col, z + d) for d in (1, -1)] + [partner]
     for other in others:
         pl.semaphore_signal(barrier, inc=1, device_id=(ctx, other), device_id_type=MESH)
@@ -435,21 +436,15 @@
         at = (k, s, piece(p))
         return remote(rs_out.at[at], rs_in.at[at], r_send.at[k, s, p], r_recv.at[k, s, p], (ctx, there))
 
-    def opposite(k):
-        p = halves(k)[0]
-        at = (k, 0, piece(p))
-        there = at_z(col, z + 2 * streams[k][1])
-        return remote(rs_out.at[at], rs_in.at[at], r_send.at[k, 0, p], r_recv.at[k, 0, p], (ctx, there))
+    far_pair = remote(far_out.at[0], far_in.at[0], r_send.at[4, 1, 0], r_recv.at[4, 1, 0], (ctx, partner))
+    far_sum = remote(far_out.at[1], far_in.at[1], r_send.at[4, 2, 0], r_recv.at[4, 2, 0], (ctx, at_z(col, z + hops + 1)))
 
     swap = remote(x_out, x_in, r_send.at[4, 0, 0], r_recv.at[4, 0, 0], (ctx, partner))
 
-    for group in (mine, theirs):
-        both = partial_of(block_at(group[0], hops + 1)).astype(BF16)
-        for k in group:
-            p = halves(k)[0]
-            rs_out[k, 0, piece(p)] = both[p * size : p * size + size]
-            opposite(k).start()
     for group, s, distance in ((theirs, 1, hops), (mine, 1, hops), (theirs, hops, 1)):
+        if s == hops:
+            far_out[0] = partial_of(block_at(theirs[0], hops + 1)).astype(BF16)
+            far_pair.start()
         for k in group:
             rs_out[k, s] = partial_of(block_at(k, distance)).astype(BF16)
         for i in range(PIECES):
@@ -467,15 +462,16 @@
                     p = halves(k)[i]
                     at = piece(p)
                     total = ready[k, at]
-                    if s == 2 and i == 0:
-                        opposite(k).wait_recv()
-                        total += rs_in[k, 0, at].astype(F32)
                     r_copy(k, s - 1, p).wait_recv()
                     rs_out[k, s, at] = (total + rs_in[k, s - 1, at].astype(F32)).astype(BF16)
                     r_copy(k, s, p).start()
 
+    ready[2] = partial_of(block_at(0, hops + 1))
     for k in mine:
         ready[k] = partial_of(block_at(k, 1))
+    far_pair.wait_recv()
+    far_out[1] = (ready[2] + far_in[0].astype(F32)).astype(BF16)
+    far_sum.start()
     for i in range(PIECES):
         for k in mine:
             p = halves(k)[i]
@@ -490,26 +486,26 @@
     long_out[...] = partial_of(tp)
     swap.wait_recv()
     long_out[...] += x_in[...].astype(F32)
+    far_sum.wait_recv()
+    long_out[...] += far_in[1].astype(F32)
     for p in range(PIECES):
         at = piece(p)
         total = long_out[at]
         for k in mine:
             r_copy(k, hops, p).wait_recv()
             total += rs_in[k, hops, at].astype(F32)
-        result[at] = total.astype(BF16)
-    done = pltpu.make_async_copy(result, out_hbm, local_sem.at[0])
-    done.start()
+        out[at] = total.astype(BF16)
 
     swap.wait_send()
     x_pair.wait_send()
+    far_pair.wait_send()
+    far_sum.wait_send()
     for k in range(4):
         g_copy(k, hops + 1, halves(k)[0]).wait_send()
-        opposite(k).wait_send()
         for p in range(PIECES):
             for s in range(1, hops + 1):
                 g_copy(k, s, p).wait_send()
                 r_copy(k, s, p).wait_send()
-    done.wait()
 
 
 def body(n_ctx, n_tp, inputs, w_in, conv_taps, pole_rates, residues, cotangent):
@@ -554,7 +550,8 @@
         vmem((4, steps - 1, rows, chans), BF16),
         vmem((rows, chans), BF16),
         vmem((rows, chans), BF16),
-        vmem((rows, chans), BF16),
+        vmem((2, rows, chans), BF16),
+        vmem((2, rows, chans), BF16),
         dma((5,)),
         dma((3,)),
         dma((5, steps, PIECES)),
@@ -567,9 +564,9 @@
     ]
     return pl.pallas_call(
         functools.partial(kernel, n_ctx, n_tp),
-        out_shape=jax.ShapeDtypeStruct((rows, chans), BF16),
+        out_shape=pltpu.VMEM((rows, chans), BF16),
         in_specs=[pl.BlockSpec(memory_space=pl.ANY)] * 6,
-        out_specs=pl.BlockSpec(memory_space=pl.ANY),
+        out_specs=pl.BlockSpec(memory_space=pltpu.VMEM),
         scratch_shapes=scratch,
         compiler_params=pltpu.CompilerParams(
             collective_id=0, has_side_effects=True, vmem_limit_bytes=60 * 1024 * 1024

time: 49.2 us -> 47.6 us (0.967); the launches traced: 49 us -> 46.7 us
  Pallas kernels: 47.5 us -> 46.1 us
  local copies, waits for them, and re-layouts: 1.47 us -> 0.63 us
    pallas_call x1, Pallas kernels: 47.5 us -> 46.1 us  [body(): pl.pallas_call(functools.partial(kernel, n_ctx, n_tp), out_shape=pltpu.VM...]
    unnamed x1, local copies, waits for them, and re-layouts: 1.47 us -> 0.63 us
where the time goes in v5:
time: 47.6 us; the launch traced here: 46.7 us
  Pallas kernels  46.1 us (97%)
  local copies, waits for them, and re-layouts  0.63 us (1%)
    pallas_call x1, Pallas kernels, body(): pl.pallas_call(functools.partial(kernel, n_ctx, n_tp), out_shape=pltpu.VM...  46.1 us

profile of v5, /device:TPU:8, one launch (start us, length us, event | category | flops | bytes accessed | tf_op | source)
XLA Modules:
  0.0 46.7 jit_solution(4365703175377214571)
XLA Ops:
  0.0 46.1 %hyena_input_grad.1 = bf16[128,256]{1,0:T(8,128)(2,1)S(1)} custom-call(bf16[128,256]{1,0:T(8,128)(2,1)} %x_hbm.1, bf16[3,4096,256]{2,1,0:T(8,128)(2,1)} %bitcast.3, f32[3,3,256]{2,1,0:T(4,128)} %taps_hbm.1, f32[16,256]{1,0:T(8,128)} %bitcast.4, f32[16,256]{1,0:T(8,128)} %bitcast.5, bf16[128,256]{1,0:T(8,128)(2,1)} %cot_hbm.1), custom_call_target="tpu_custom_call" | custom-call | flops 1610612736 | bytes 6291456 | tf_op jit(solution)/shard_map/hyena_input_grad/pallas_call | solution.py:565
  46.1 0.6 %copy.8 = bf16[128,256]{1,0:T(8,128)(2,1)} copy(bf16[128,256]{1,0:T(8,128)(2,1)S(1)} %hyena_input_grad.1) | data formatting | bytes 131072

commit v6 on v5

--- a/solution.py
+++ b/solution.py
@@ -126,8 +126,6 @@
             ((x_hbm, xg.at[tp]), (taps_hbm, taps), (rate_hbm, rate), (res_hbm, res), (cot_hbm, cot))
         )
     ]
-    for c in small + w_copies:
-        c.start()
     pl.semaphore_wait(barrier, len(others) + rounds)
 
     def remote(src, dst, send, recv, device):
@@ -177,6 +175,8 @@
         for k in mine:
             g_copy(k, 1, halves(k)[i]).start()
     x_pair.start()
+    for c in small + w_copies:
+        c.start()
     greet(0)
 
     for c in small[1:]:
@@ -212,19 +212,12 @@
             proj[j, SUB:, :] = total
 
     proj[...] = jnp.zeros_like(proj)
-    small[0].wait()
-    for c in w_copies:
-        c.wait()
-    project([tp])
-    per_step = -(-poles // hops)
-    ctx_per_step = -(-n_ctx // hops)
-
-    def beside(s):
-        greeted(s - 1)
-        greet(s)
-        lax.fori_loop((s - 1) * per_step, min(s * per_step, poles), tables, 0)
-        lax.fori_loop((s - 1) * ctx_per_step, min(s * ctx_per_step, n_ctx), state_weights, 0)
-
+    def all_tables(part):
+        half_poles, half_ctx = poles // 2, n_ctx // 2
+        lax.fori_loop(part * half_poles, (part + 1) * half_poles, tables, 0)
+        lax.fori_loop(part * half_ctx, (part + 1) * half_ctx, state_weights, 0)
+
+    all_tables(0)
     for i in range(PIECES):
         for k in mine:
             forward(k, 1, i)
@@ -232,41 +225,49 @@
     for i in range(PIECES):
         for k in theirs:
             g_copy(k, 1, halves(k)[i]).start()
-    project([block_at(k, -1) for k in mine])
-    beside(1)
+    small[0].wait()
+    for c in w_copies:
+        c.wait()
+    project([tp] + [block_at(k, -1) for k in mine])
+    greeted(0)
+    greet(1)
     for s in range(2, hops):
         for group in (mine, theirs):
             for i in range(PIECES):
                 for k in group:
                     forward(k, s, i)
         project([block_at(k, -s) for k in range(4)])
-        beside(s)
+        greeted(s - 1)
+        greet(s)
+    all_tables(1)
+    def spread_rows(i, _):
+        block = kern[pl.ds(pl.multiple_of(SUB * i, SUB), SUB), :]
+        for r in range(SUB):
+            spread[SUB * i + r] = jnp.broadcast_to(block[r : r + 1, :], (SUB, chans))
+        return 0
+
+    lax.fori_loop(0, rows // SUB, spread_rows, 0)
+    kern_late[0:1, :] = jnp.zeros((1, chans), F32)
+    kern_late[1:rows, :] = kern[0 : rows - 1, :]
+
     x_pair.wait_recv()
     for k in mine:
         for i in range(PIECES):
             forward(k, hops, i)
     project([block_at(k, -hops) for k in mine] + [partner])
-    beside(hops)
+    greeted(hops - 1)
+    greet(hops)
     for k in theirs:
         for i in range(PIECES):
             arrived(k, 1, halves(k)[i])
-    project([block_at(k, -1) for k in theirs])
+    for k in mine:
+        arrived(k, hops + 1, halves(k)[0])
+    project([block_at(k, -1) for k in theirs] + [block_at(0, hops + 1)])
     for k in theirs:
         for i in range(PIECES):
             forward(k, hops, i)
-    for k in range(4):
         arrived(k, hops + 1, halves(k)[0])
-    project([block_at(k, -hops) for k in theirs] + [block_at(0, hops + 1), block_at(2, hops + 1)])
-
-    def spread_rows(i, _):
-        block = kern[pl.ds(pl.multiple_of(SUB * i, SUB), SUB), :]
-        for r in range(SUB):
-            spread[SUB * i + r] = jnp.broadcast_to(block[r : r + 1, :], (SUB, chans))
-        return 0
-
-    lax.fori_loop(0, rows // SUB, spread_rows, 0)
-    kern_late[0:1, :] = jnp.zeros((1, chans), F32)
-    kern_late[1:rows, :] = kern[0 : rows - 1, :]
+    project([block_at(k, -hops) for k in theirs] + [block_at(2, hops + 1)])
 
     for j in range(3):
         proj[j, SUB:, :] = proj[j, SUB:, :].astype(BF16).astype(F32)

time: 47.6 us -> 46.9 us (0.985); the launches traced: 46.7 us -> 46.9 us
  no operation moved by 1% of the time
where the time goes in v6:
time: 46.9 us
  Pallas kernels  46.2 us (99%)
  local copies, waits for them, and re-layouts  0.63 us (1%)
    pallas_call x1, Pallas kernels, body(): pl.pallas_call(functools.partial(kernel, n_ctx, n_tp), out_shape=pltpu.VM...  46.2 us

profile of v6, /device:TPU:8, one launch (start us, length us, event | category | flops | bytes accessed | tf_op | source)
XLA Modules:
  0.0 46.9 jit_solution(3766136467728029841)
XLA Ops:
  0.0 46.2 %hyena_input_grad.1 = bf16[128,256]{1,0:T(8,128)(2,1)S(1)} custom-call(bf16[128,256]{1,0:T(8,128)(2,1)} %x_hbm.1, bf16[3,4096,256]{2,1,0:T(8,128)(2,1)} %bitcast.3, f32[3,3,256]{2,1,0:T(4,128)} %taps_hbm.1, f32[16,256]{1,0:T(8,128)} %bitcast.4, f32[16,256]{1,0:T(8,128)} %bitcast.5, bf16[128,256]{1,0:T(8,128)(2,1)} %cot_hbm.1), custom_call_target="tpu_custom_call" | custom-call | flops 1610612736 | bytes 6291456 | tf_op jit(solution)/shard_map/hyena_input_grad/pallas_call | solution.py:566
  46.2 0.6 %copy.8 = bf16[128,256]{1,0:T(8,128)(2,1)} copy(bf16[128,256]{1,0:T(8,128)(2,1)S(1)} %hyena_input_grad.1) | data formatting | bytes 131072

commit v7 on v6

--- a/solution.py
+++ b/solution.py
@@ -104,8 +104,7 @@
         return ctx + 2**r * (1 - 2 * bit)
 
     barrier = pltpu.get_barrier_semaphore()
-    others = [at_z(col, z + d) for d in (1, -1, 2, -2, hops + 1)]
-    others += [at_z(1 - col, z + d) for d in (1, -1)] + [partner]
+    others = [at_z(col, z + 1), at_z(col, z - 1), partner]
     for other in others:
         pl.semaphore_signal(barrier, inc=1, device_id=(ctx, other), device_id_type=MESH)
     for r in range(rounds):
@@ -221,6 +220,7 @@
     for i in range(PIECES):
         for k in mine:
             forward(k, 1, i)
+        for k in mine:
             g_copy(k + 2, 2, halves(k)[i]).start()
     for i in range(PIECES):
         for k in theirs:
@@ -293,14 +293,18 @@
     glp[0:rows, :] = jnp.where(steps >= 2.0, cot[...].astype(F32) * filtered[0], 0.0)
     glp[rows : rows + SUB, :] = jnp.zeros((SUB, chans), F32)
 
-    def partial_states(n, _):
-        fwd = rev_pow[n] * mixp[SUB:, :]
-        bwd = fwd_pow[n] * glp[0:rows, :]
-        part[0, n] = jnp.sum(fwd.reshape(rows // SUB, SUB, chans), axis=0)
-        part[1, n] = jnp.sum(bwd.reshape(rows // SUB, SUB, chans), axis=0)
-        return 0
-
-    lax.fori_loop(0, poles, partial_states, 0)
+    for lane in range(0, chans, LANES):
+        cols = slice(lane, lane + LANES)
+        mix_now, gl_now = mixp[SUB:, cols], glp[0:rows, cols]
+
+        def partial_states(n, _, cols=cols, mix_now=mix_now, gl_now=gl_now):
+            fwd = rev_pow[n, :, cols] * mix_now
+            bwd = fwd_pow[n, :, cols] * gl_now
+            part[0, n, :, cols] = jnp.sum(fwd.reshape(rows // SUB, SUB, LANES), axis=0)
+            part[1, n, :, cols] = jnp.sum(bwd.reshape(rows // SUB, SUB, LANES), axis=0)
+            return 0
+
+        lax.fori_loop(0, poles, partial_states, 0, unroll=2)
     ends[0] = gain[...] * jnp.sum(part[0], axis=1)
     ends[1] = jnp.sum(part[1], axis=1)
     state[0, 0:poles, :] = ends[0].astype(BF16)

time: 46.9 us -> 46.2 us (0.985)
  Pallas kernels: 46.2 us -> 45.1 us
    pallas_call x1, Pallas kernels: 46.2 us -> 45.1 us  [body(): pl.pallas_call(functools.partial(kernel, n_ctx, n_tp), out_shape=pltpu.VM...]
where the time goes in v7:
time: 46.2 us; the launch traced here: 45.7 us
  Pallas kernels  45.1 us (98%)
  local copies, waits for them, and re-layouts  0.63 us (1%)
    pallas_call x1, Pallas kernels, body(): pl.pallas_call(functools.partial(kernel, n_ctx, n_tp), out_shape=pltpu.VM...  45.1 us

profile of v7, /device:TPU:8, one launch (start us, length us, event | category | flops | bytes accessed | tf_op | source)
XLA Modules:
  0.0 45.7 jit_solution(14728370712964384287)
XLA Ops:
  0.0 45.1 %hyena_input_grad.1 = bf16[128,256]{1,0:T(8,128)(2,1)S(1)} custom-call(bf16[128,256]{1,0:T(8,128)(2,1)} %x_hbm.1, bf16[3,4096,256]{2,1,0:T(8,128)(2,1)} %bitcast.3, f32[3,3,256]{2,1,0:T(4,128)} %taps_hbm.1, f32[16,256]{1,0:T(8,128)} %bitcast.4, f32[16,256]{1,0:T(8,128)} %bitcast.5, bf16[128,256]{1,0:T(8,128)(2,1)} %cot_hbm.1), custom_call_target="tpu_custom_call" | custom-call | flops 1610612736 | bytes 6291456 | tf_op jit(solution)/shard_map/hyena_input_grad/pallas_call | solution.py:570
  45.1 0.6 %copy.8 = bf16[128,256]{1,0:T(8,128)(2,1)} copy(bf16[128,256]{1,0:T(8,128)(2,1)S(1)} %hyena_input_grad.1) | data formatting | bytes 131072

commit v8 on v7

--- a/solution.py
+++ b/solution.py
@@ -212,9 +212,9 @@
 
     proj[...] = jnp.zeros_like(proj)
     def all_tables(part):
-        half_poles, half_ctx = poles // 2, n_ctx // 2
-        lax.fori_loop(part * half_poles, (part + 1) * half_poles, tables, 0)
-        lax.fori_loop(part * half_ctx, (part + 1) * half_ctx, state_weights, 0)
+        first_poles, first_ctx = poles * 4 // 16, n_ctx * 4 // 16
+        lax.fori_loop(*((0, first_poles), (first_poles, poles))[part], tables, 0)
+        lax.fori_loop(*((0, first_ctx), (first_ctx, n_ctx))[part], state_weights, 0)
 
     all_tables(0)
     for i in range(PIECES):

time: 46.2 us -> 45.8 us (level)
  no operation moved by 1% of the time
where the time goes in v8:
time: 45.8 us; the launch traced here: 45.7 us
  Pallas kernels  45 us (98%)
  local copies, waits for them, and re-layouts  0.63 us (1%)
    pallas_call x1, Pallas kernels, body(): pl.pallas_call(functools.partial(kernel, n_ctx, n_tp), out_shape=pltpu.VM...  45 us

profile of v8, /device:TPU:8, one launch (start us, length us, event | category | flops | bytes accessed | tf_op | source)
XLA Modules:
  0.0 45.7 jit_solution(2995983530002319350)
XLA Ops:
  0.0 45.0 %hyena_input_grad.1 = bf16[128,256]{1,0:T(8,128)(2,1)S(1)} custom-call(bf16[128,256]{1,0:T(8,128)(2,1)} %x_hbm.1, bf16[3,4096,256]{2,1,0:T(8,128)(2,1)} %bitcast.3, f32[3,3,256]{2,1,0:T(4,128)} %taps_hbm.1, f32[16,256]{1,0:T(8,128)} %bitcast.4, f32[16,256]{1,0:T(8,128)} %bitcast.5, bf16[128,256]{1,0:T(8,128)(2,1)} %cot_hbm.1), custom_call_target="tpu_custom_call" | custom-call | flops 1610612736 | bytes 6291456 | tf_op jit(solution)/shard_map/hyena_input_grad/pallas_call | solution.py:570
  45.0 0.6 %copy.8 = bf16[128,256]{1,0:T(8,128)(2,1)} copy(bf16[128,256]{1,0:T(8,128)(2,1)S(1)} %hyena_input_grad.1) | data formatting | bytes 131072

commit v9 on v8

--- a/solution.py
+++ b/solution.py
@@ -471,12 +471,12 @@
                     rs_out[k, s, at] = (total + rs_in[k, s - 1, at].astype(F32)).astype(BF16)
                     r_copy(k, s, p).start()
 
-    ready[2] = partial_of(block_at(0, hops + 1))
+    total = partial_of(block_at(0, hops + 1))
+    far_pair.wait_recv()
+    far_out[1] = (total + far_in[0].astype(F32)).astype(BF16)
+    far_sum.start()
     for k in mine:
         ready[k] = partial_of(block_at(k, 1))
-    far_pair.wait_recv()
-    far_out[1] = (ready[2] + far_in[0].astype(F32)).astype(BF16)
-    far_sum.start()
     for i in range(PIECES):
         for k in mine:
             p = halves(k)[i]

time: 45.8 us -> 45.7 us (level)
  no operation moved by 1% of the time
where the time goes in v9:
time: 45.7 us
  Pallas kernels  45 us (98%)
  local copies, waits for them, and re-layouts  0.63 us (1%)
    pallas_call x1, Pallas kernels, body(): pl.pallas_call(functools.partial(kernel, n_ctx, n_tp), out_shape=pltpu.VM...  45 us

profile of v9, /device:TPU:8, one launch (start us, length us, event | category | flops | bytes accessed | tf_op | source)
XLA Modules:
  0.0 45.7 jit_solution(6000260078527131807)
XLA Ops:
  0.0 45.0 %hyena_input_grad.1 = bf16[128,256]{1,0:T(8,128)(2,1)S(1)} custom-call(bf16[128,256]{1,0:T(8,128)(2,1)} %x_hbm.1, bf16[3,4096,256]{2,1,0:T(8,128)(2,1)} %bitcast.3, f32[3,3,256]{2,1,0:T(4,128)} %taps_hbm.1, f32[16,256]{1,0:T(8,128)} %bitcast.4, f32[16,256]{1,0:T(8,128)} %bitcast.5, bf16[128,256]{1,0:T(8,128)(2,1)} %cot_hbm.1), custom_call_target="tpu_custom_call" | custom-call | flops 1610612736 | bytes 6291456 | tf_op jit(solution)/shard_map/hyena_input_grad/pallas_call | solution.py:570
  45.0 0.6 %copy.8 = bf16[128,256]{1,0:T(8,128)(2,1)} copy(bf16[128,256]{1,0:T(8,128)(2,1)S(1)} %hyena_input_grad.1) | data formatting | bytes 131072
